TPU v7x, 32 devices: a whole 2x2x4 slice. The times are simulated.
32 devices in a mesh: groups: 2 (over x), expert: 16 (over z, y, core), dp: 1.
Axes of the slice: x: 2, y: 2, z: 4, core: 2. Of those that a mesh axis runs over, the one named last changes fastest.
Arguments:
- token_codes: bfloat16 [2048, 4096], P(('groups', 'expert', 'dp')), parts along dimension 0, may hold values from -6 to 6
- token_scales: bfloat16 [2048, 32], P(('groups', 'expert', 'dp')), parts along dimension 0, may hold values from 0.25 to 4
- expert_ids: int32 [2048, 8], P(('groups', 'expert', 'dp')), parts along dimension 0, may hold values from 0 to 15, all different within a row; in each aligned block of 64 rows (0 to 63, 64 to 127, ...) at most 48 rows name the same one
- gate_values: float32 [2048, 8], P(('groups', 'expert', 'dp')), parts along dimension 0, may hold values from 0.05 to 0.25
- w_gate: bfloat16 [16, 4096, 1536], P('expert', None, 'dp'), may hold values from -0.09375 to 0.09375
- w_up: bfloat16 [16, 4096, 1536], P('expert', None, 'dp'), may hold values from -0.09375 to 0.09375
- w_down: bfloat16 [16, 1536, 4096], P('expert', 'dp'), may hold values from -0.15625 to 0.15625
- gate_scales: float32 [16, 32, 12], P('expert', None, 'dp'), may hold values from 0.5 to 2
- up_scales: float32 [16, 32, 12], P('expert', None, 'dp'), may hold values from 0.5 to 2
- down_scales: float32 [16, 12, 32], P('expert', 'dp'), may hold values from 0.5 to 2
Outputs:
- mixed: bfloat16 [2048, 4096], P(('groups', 'expert', 'dp')), parts along dimension 0
There are 2 independent parts, one for each index of `groups`. A program takes and returns all parts, laid end to end along the dimension named above; an argument that names none is the same for every part. Nothing has to cross between parts.
Inputs may be any that keep to these rules, and one draw needn't show every extreme that they name: `expert_ids`: each token names 8 different experts. Among the 64 tokens of one device no expert is named by more than 48 tokens, and in every draw some device names some expert in exactly 48 tokens.
All inputs are finite; a program needn't handle non-finite values.
Results may differ from a plain program's by a relative error of at most 0.028.
Values may be sent and summed in bfloat16 or wider, within the bound.
No kernel may reach another device: no remote copies, remote signals or barrier semaphores. Data moves between devices by JAX's collectives and lax.ppermute only.
A program may use at most 320 MiB of HBM per device.

v0:
```python
import functools

import jax
import jax.numpy as jnp
from jax import lax
from jax.experimental import pallas as pl
from jax.experimental.pallas import tpu as pltpu
from jax.sharding import PartitionSpec as P

BF16 = jnp.bfloat16
F32 = jnp.float32
TILE_FF = 256
TILE_D = 512
SLOT_BYTES = 5 << 20
PARTS_FF, PARTS_D = 2, 4
HID, DEQ = 3, 6
COST = 1024
MB = 1 << 20


def whole(space=pltpu.VMEM):
    return pl.BlockSpec(memory_space=space)


def ordered(kernel, operands, in_specs, out_shape, waits, *, holds=(), scratch=(), flops, moved, vmem, name):
    count, extra = len(operands), len(waits) + len(holds)

    def body(*refs):
        refs = [*refs[:count], *refs[count + extra :]]
        mark = refs.pop(count + len(out_shape))
        mark[...] = jnp.zeros_like(mark)
        kernel(*refs)

    return pl.pallas_call(
        body,
        in_specs=[*in_specs, *[whole(pl.ANY)] * len(waits), *[whole()] * len(holds)],
        out_specs=[whole()] * (len(out_shape) + 1),
        out_shape=[*out_shape, jax.ShapeDtypeStruct((8, 128), F32)],
        scratch_shapes=scratch,
        cost_estimate=pl.CostEstimate(flops=flops, bytes_accessed=moved, transcendentals=0),
        compiler_params=pltpu.CompilerParams(vmem_limit_bytes=vmem * MB),
        name=name,
    )(*operands, *waits, *holds)


def prep_kernel(codes_ref, scales_ref, ids_ref, gates_ref, out_ref, *, experts):
    count, width = codes_ref.shape
    scales = scales_ref[...].astype(F32).T
    for b in range(width // 128):
        columns = pl.ds(b * 128, 128)
        out_ref[:, columns] = (codes_ref[:, columns].astype(F32) * scales[:, b : b + 1]).astype(BF16)
    row = lax.broadcasted_iota(jnp.int32, (128, count), 0)
    expert = row % experts
    dense = jnp.zeros((128, count), F32)
    for k in range(ids_ref.shape[0]):
        dense = dense + jnp.where(ids_ref[k : k + 1, :] == expert, gates_ref[k : k + 1, :], 0.0)
    high = dense.astype(BF16).astype(F32)
    both = jnp.where(row < experts, high, jnp.where(row < 2 * experts, dense - high, 0.0))
    out_ref[:, pl.ds(width, 128)] = both.T.astype(BF16)


def prep(codes, scales, ids, gates, experts):
    count, width = codes.shape
    return pl.pallas_call(
        functools.partial(prep_kernel, experts=experts),
        in_specs=[whole()] * 4,
        out_specs=whole(),
        out_shape=pltpu.VMEM((count, width + 128), BF16),
        cost_estimate=pl.CostEstimate(flops=count * width, bytes_accessed=4 * count * width, transcendentals=0),
        name="prep",
    )(codes, scales.T, ids.T, gates.T)


def dequant_kernel(*refs, count, by_row, parts):
    all_scales, weights, refs = refs[:count], refs[count : 2 * count], refs[2 * count :]
    outs, slots, sems = refs[: count * parts], refs[count * parts : count * (parts + 1)], refs[count * (parts + 1) :]
    steps = weights[0].shape[0] // 128
    depth, _, breadth = slots[0].shape
    tiles, _, tile = outs[0].shape
    ahead = min(depth - 1, steps)

    def copy(m, i):
        slot = lax.rem(i, depth)
        source = weights[m].at[pl.ds(pl.multiple_of(i * 128, 128), 128)]
        return pltpu.make_async_copy(source, slots[m].at[slot], sems[m].at[slot])

    for i in range(ahead):
        for m in range(count):
            copy(m, i).start()

    @pl.loop(0, steps)
    def _(i):
        for m in range(count):

            @pl.when(i + ahead < steps)
            def _():
                copy(m, i + ahead).start()

            copy(m, i).wait()
            for j in range(breadth // 128):
                value = all_scales[m][i, 0, j] if by_row else all_scales[m][j, 0, i]
                block = slots[m][lax.rem(i, depth), :, pl.ds(j * 128, 128)].astype(F32) * value
                part, n = divmod(j * 128 // tile, tiles)
                at = pl.ds(pl.multiple_of(i * 128, 128), 128)
                outs[m * parts + part][n, at, pl.ds(j * 128 % tile, 128)] = block.astype(BF16)


def dequant(weights, scales, by_row, tile, parts, waits, name):
    count = len(weights)
    weights = [pltpu.with_memory_space_constraint(w, pltpu.HBM) for w in weights]
    height, breadth = weights[0].shape
    slots = max(2, min(SLOT_BYTES // (256 * breadth * count), height // 128))
    size = count * height * breadth
    while breadth // tile % parts:
        parts -= 1
    *mats, mark = ordered(
        functools.partial(dequant_kernel, count=count, by_row=by_row, parts=parts),
        [*scales, *weights],
        [whole(pltpu.SMEM)] * count + [whole(pltpu.HBM)] * count,
        [pltpu.VMEM((breadth // tile // parts, height, tile), BF16)] * (count * parts),
        waits,
        scratch=[
            *[pltpu.VMEM((slots, 128, breadth), BF16)] * count,
            *[pltpu.SemaphoreType.DMA((slots,))] * count,
        ],
        flops=COST * size,
        moved=4 * size,
        vmem=DEQ,
        name=name,
    )
    return [mats[m * parts : (m + 1) * parts] for m in range(count)], mark


def hidden_kernel(*refs, experts, count):
    blocks, gates, ups = refs[: -2 * count - 2], refs[-2 * count - 2 : -count - 2], refs[-count - 2 : -2]
    hidden_ref, rows_ref = refs[-2:]
    tiles, width, tile = gates[0].shape
    at = 0
    for block in blocks:
        rows_ref[pl.ds(at, block.shape[0]), :] = block[...]
        at += block.shape[0]
    sent = rows_ref[:, pl.ds(width, 128)].astype(F32)
    lane = lax.broadcasted_iota(jnp.int32, sent.shape, 1)
    mine = lax.axis_index("expert")
    value = jnp.sum(jnp.where((lane == mine) | (lane == mine + experts), sent, 0.0), axis=1, keepdims=True)

    @pl.loop(0, tiles)
    def _(n):
        for part in range(count):
            rows = rows_ref[:, pl.ds(0, width)]
            gated = jnp.dot(rows, gates[part][n], preferred_element_type=F32)
            upward = jnp.dot(rows, ups[part][n], preferred_element_type=F32)
            columns = pl.ds(pl.multiple_of((part * tiles + n) * tile, tile), tile)
            hidden_ref[:, columns] = (gated / (1.0 + jnp.exp(-gated)) * upward * value).astype(BF16)


def hidden_of(blocks, gates, ups, experts, waits, name):
    rows = sum(b.shape[0] for b in blocks)
    tiles, width, tile = gates[0].shape
    depth = len(gates) * tiles * tile
    return ordered(
        functools.partial(hidden_kernel, experts=experts, count=len(gates)),
        [*blocks, *gates, *ups],
        [whole()] * (len(blocks) + 2 * len(gates)),
        [pltpu.VMEM((rows, depth), BF16)],
        waits,
        scratch=[pltpu.VMEM((rows, width + 128), BF16)],
        flops=2 * rows * width * depth,
        moved=2 * rows * width,
        vmem=HID,
        name=name,
    )


def down_kernel(hidden_ref, *refs):
    *mats, mine_ref, theirs_ref = refs
    tiles, _, tile = mats[0].shape
    half = mine_ref.shape[0]

    @pl.loop(0, tiles)
    def _(n):
        for part in range(len(mats)):
            out = jnp.dot(hidden_ref[...], mats[part][n], preferred_element_type=F32).astype(BF16)
            columns = pl.ds(pl.multiple_of((part * tiles + n) * tile, tile), tile)
            mine_ref[:, columns] = out[:half]
            theirs_ref[:, columns] = out[half:]


def down_of(hidden, mats, waits, name):
    count, depth = hidden.shape
    tiles, _, tile = mats[0].shape
    width = len(mats) * tiles * tile
    return ordered(
        down_kernel,
        [hidden, *mats],
        [whole()] * (1 + len(mats)),
        [pltpu.VMEM((count // 2, width), BF16), jax.ShapeDtypeStruct((count // 2, width), BF16)],
        waits,
        flops=1,
        moved=1,
        vmem=1,
        name=name,
    )


def totals_kernel(*refs, plan):
    outs = refs[len(refs) - len(plan) :]
    for out, blocks in zip(outs, plan, strict=True):
        size = out.shape[0] // len(blocks)
        for n, terms in enumerate(blocks):
            total = sum(refs[i][pl.ds(at, size), :].astype(F32) for i, at in terms)
            out[pl.ds(n * size, size), :] = total.astype(BF16)


def totals(arrays, size, plan, waits=(), name="totals"):
    width = arrays[0].shape[1]
    rows = size * sum(map(len, plan))
    return ordered(
        functools.partial(totals_kernel, plan=plan),
        arrays,
        [whole()] * len(arrays),
        [jax.ShapeDtypeStruct((size * len(blocks), width), BF16) for blocks in plan],
        waits,
        flops=1,
        moved=1,
        vmem=1,
        name=name,
    )


def after(value, mark):
    return lax.optimization_barrier((value, mark))


def solution(mesh):
    experts, pairs = mesh.shape["expert"], mesh.shape["dp"]
    chips = experts * pairs // 2
    if pairs == 1:
        walk = [*range(0, chips, 2), *reversed(range(1, chips, 2))]
    else:
        walk = [*range(chips)]
    far = chips // 2
    names = ("expert", "dp")

    def shift(k):
        return [
            (2 * walk[p] + core, 2 * walk[(p + k) % chips] + core)
            for p in range(chips)
            for core in range(2)
        ]

    def right(a):
        return lax.ppermute(a, names, shift(1))

    def left(a):
        return lax.ppermute(a, names, shift(-1))

    def across(a):
        return lax.ppermute(a, names, [(i, i ^ 1) for i in range(2 * chips)])

    def shards(codes, scales, ids, gates, w_gate, w_up, w_down, gate_scales, up_scales, down_scales):
        block = prep(codes, scales, ids, gates, experts)
        count = block.shape[0]
        half = count // 2

        l = left(block)
        r = right(block)
        home = [block, across(block)]
        (gate_mats, up_mats), mark = dequant(
            [w_gate[0], w_up[0]],
            [gate_scales.transpose(2, 0, 1), up_scales.transpose(2, 0, 1)],
            False,
            TILE_FF,
            PARTS_FF,
            [block],
            "dequant_both",
        )
        hiddens = []

        def hide(blocks, waits):
            hidden, mark = hidden_of(blocks, gate_mats, up_mats, experts, waits, f"H{len(hiddens)}")
            hiddens.append(hidden)
            return mark

        for k in range(1, far + 1):
            (r, l), mark = after((r, l), mark)
            first, second = [((0, 0),), ((0, half),)], [((1, 0),), ((1, half),)]
            if k < far - 1:
                both, mark = totals([r, l], half, [[*first, *second]], [mark])
                l = left(l)
                r = right(r)
            elif k < far:
                r, l, both, mark = totals([r, l], half, [first[:1], second[1:], [*first, *second]], [mark])
                l = left(l)
                r = right(r)
            else:
                both, mark = totals([r, l], half, [[first[0], second[0]]], [mark])
            blocks = [both, across(both)]
            if k == 1:
                mark = hide(home, [mark])
            if k == min(2, far):
                (down_mats,), mark = dequant(
                    [w_down[0]],
                    [down_scales.transpose(1, 0, 2)],
                    True,
                    TILE_D,
                    PARTS_D,
                    [mark],
                    "dequant_down",
                )
            if k == far:
                *upper, mark = down_of(hiddens[-1], down_mats, [mark], f"D{k - 1}")
            mark = hide(blocks, [mark])

        def down(k, waits):
            mine, theirs, mark = down_of(hiddens[k], down_mats, waits, f"D{k}")
            return [mine, across(theirs)], mark

        def sums(name, pair, received, rows_r, rows_l, waits=()):
            own = [((0, at), (1, at)) for at in (rows_r, rows_l)]
            if received:
                own = [(*own[0], (2, 0)), (*own[1], (3, 0))]
            *both, mark = totals([*pair, *received], half, [[terms] for terms in own], waits, name)
            return both, mark

        def move(pair):
            return [right(pair[0]), left(pair[1])]

        pairs = {far - 1: [upper[0], across(upper[1])]}
        short, mark = sums(f"S{far - 1}", pairs[far - 1], [], count, half)
        short = move(short)
        pairs[far], mark = down(far, [mark])
        for k in range(far - 2, -1, -1):
            pairs[k], mark = down(k, [mark])
        long = []
        for k in range(far - 2, -1, -1):
            at = (count + half, 0) if long else (half, 0)
            long, mark = sums(f"L{k + 2}", pairs[k + 2], long, *at, [mark])
            long = move(long)
            if k > 0:
                short, mark = sums(f"S{k}", pairs[k], short, count, half, [mark])
                short = move(short)
        long, _ = sums("L1", pairs[1], long, count + half, 0, [mark])
        long = move(long)
        arrays = [*pairs[0], *short, *long]
        plan = [((0, 0), (1, 0), (2, 0), (5, 0)), ((0, half), (1, half), (3, 0), (4, 0))]
        return totals(arrays, half, [plan])[0]

    token = P(("groups", "expert", "dp"), None)
    return jax.shard_map(
        shards,
        mesh=mesh,
        in_specs=(
            token,
            token,
            token,
            token,
            P("expert", None, "dp"),
            P("expert", None, "dp"),
            P("expert", "dp", None),
            P("expert", None, "dp"),
            P("expert", None, "dp"),
            P("expert", "dp", None),
        ),
        out_specs=token,
        check_vma=False,
    )
```

profile of v0, /device:TPU:0, one launch (start us, length us, event | category | flops | bytes accessed | tf_op | source)
XLA Modules:
  0.0 129.3 jit_solution(16537925830094508091)
XLA Ops:
  0.0 1.4 %prep.1.refs_4_.refs_0_ = bf16[64,4224]{1,0:T(8,128)(2,1)S(1)} custom-call(bf16[64,4096]{1,0:T(8,128)(2,1)} %codes_ref.1, bf16[32,64]{1,0:T(8,128)(2,1)} %bitcast.12, s32[8,64]{1,0:T(8,128)} %bitcast.13, f32[8,64]{1,0:T(8,128)} %bitcast.14), custom_call_target="tpu_custom_call" | custom-call | flops 262144 | bytes 1048576 | tf_op jit(solution)/shard_map/prep/pallas_call | solution.py:64
  1.4 3.0 %collective-permute-start.2 = (bf16[64,4224]{1,0:T(8,128)(2,1)S(1)}, bf16[64,4224]{1,0:T(8,128)(2,1)S(1)}, u32[]{:S(2)}, u32[]{:S(2)}) collective-permute-start(bf16[64,4224]{1,0:T(8,128)(2,1)S(1)} %prep.1.refs_4_.refs_0_), channel_id=1, source_target_pairs={{0,2},{1,3},{4,0},{5,1},{8,4},{9,5},{12,8},{13,9},{14,12},{15,13},... | collective-permute-start | bytes 1622024 | tf_op jit(solution)/shard_map/ppermute | solution.py:256
  4.6 0.7 copy-done
  5.3 0.7 copy-done.1
  6.0 9.6 %dequant_both.1 = (bf16[3,4096,256]{2,1,0:T(8,128)(2,1)S(1)}, bf16[3,4096,256]{2,1,0:T(8,128)(2,1)S(1)}, bf16[3,4096,256]{2,1,0:T(8,128)(2,1)S(1)}, bf16[3,4096,256]{2,1,0:T(8,128)(2,1)S(1)}, f32[8,128]{1,0:T(8,128)S(1)}) custom-call(f32[12,1,32]{2,1,0:T(1,128)S(1)} %bitcast.9, f32[12,1,32]{2,1,0:T(1,128)S(1)} %bitcast.10, bf16[4096,1536]{1,0:T(8,128)(2,1)} %bitcast.15, ...), custom_call_target="tpu_custom_call" | custom-call | flops 12884901888 | bytes 50331648 | tf_op jit(solution)/shard_map/dequant_both/pallas_call | solution.py:34
  15.6 1.2 collective-permute-done.2.refs_1_
  16.8 1.4 %collective-permute-done.1.refs_0_ = bf16[64,4224]{1,0:T(8,128)(2,1)S(1)} collective-permute-done((bf16[64,4224]{1,0:T(8,128)(2,1)S(1)}, bf16[64,4224]{1,0:T(8,128)(2,1)S(1)}, u32[]{:S(2)}, u32[]{:S(2)}) %collective-permute-start.1) | collective-permute-done | bytes 540704 | tf_op jit(solution)/shard_map/ppermute | solution.py:253
  19.3 1.6 %collective-permute-start.4 = (bf16[64,4224]{1,0:T(8,128)(2,1)S(1)}, bf16[64,4224]{1,0:T(8,128)(2,1)S(1)}, u32[]{:S(2)}, u32[]{:S(2)}) collective-permute-start(bf16[64,4224]{1,0:T(8,128)(2,1)S(1)} %collective-permute-done.2.refs_1_), channel_id=1, source_target_pairs={{0,2},{1,3},{4,0},{5,1},{8,4},{9,5},{12,8},{13,9},{14,12},{15,13},... | collective-permute-start | bytes 1622024 | tf_op jit(solution)/shard_map/ppermute | solution.py:256
  20.9 0.9 collective-permute-done.refs_1_
  21.8 4.2 %H0.1 = (bf16[128,1536]{1,0:T(8,128)(2,1)S(1)}, f32[8,128]{1,0:T(8,128)S(1)}) custom-call(bf16[64,4224]{1,0:T(8,128)(2,1)S(1)} %prep.1.refs_4_.refs_0_, bf16[64,4224]{1,0:T(8,128)(2,1)S(1)} %collective-permute-done.refs_1_, bf16[3,4096,256]{2,1,0:T(8,128)(2,1)S(1)} %get-tuple-element.82.refs_2_, bf16[3,4096,256]{2,1,0:T(8,128)(2,1)S(1)} %get-tuple-element.83.refs_3_, ...), custom_call_target="tpu_custom_call" | custom-call | flops 1610612736 | bytes 1048576 | tf_op jit(solution)/shard_map/H0/pallas_call | solution.py:34
  26.0 7.3 %H1.1 = (bf16[256,1536]{1,0:T(8,128)(2,1)S(1)}, f32[8,128]{1,0:T(8,128)S(1)}) custom-call(bf16[128,4224]{1,0:T(8,128)(2,1)S(1)} %get-tuple-element.92.refs_0_, bf16[128,4224]{1,0:T(8,128)(2,1)S(1)} %collective-permute-done.5.refs_1_, bf16[3,4096,256]{2,1,0:T(8,128)(2,1)S(1)} %get-tuple-element.82.refs_2_, ...), custom_call_target="tpu_custom_call" | custom-call | flops 3221225472 | bytes 2097152 | tf_op jit(solution)/shard_map/H1/pallas_call | solution.py:34
  33.7 1.4 %collective-permute-start.7 = (bf16[64,4224]{1,0:T(8,128)(2,1)S(1)}, bf16[64,4224]{1,0:T(8,128)(2,1)S(1)}, u32[]{:S(2)}, u32[]{:S(2)}) collective-permute-start(bf16[64,4224]{1,0:T(8,128)(2,1)S(1)} %collective-permute-done.3.refs_0_), channel_id=1, source_target_pairs={{0,4},{1,5},{4,8},{5,9},{8,12},{9,13},{12,14},{13,15},{14,10},{15,... | collective-permute-start | bytes 1622024 | tf_op jit(solution)/shard_map/ppermute | solution.py:253
  35.1 0.6 collective-permute-start.8
  35.7 5.8 %dequant_down.1 = (bf16[2,1536,512]{2,1,0:T(8,128)(2,1)S(1)}, bf16[2,1536,512]{2,1,0:T(8,128)(2,1)S(1)}, bf16[2,1536,512]{2,1,0:T(8,128)(2,1)S(1)}, bf16[2,1536,512]{2,1,0:T(8,128)(2,1)S(1)}, f32[8,128]{1,0:T(8,128)S(1)}) custom-call(f32[12,1,32]{2,1,0:T(1,128)S(1)} %bitcast.11, bf16[1536,4096]{1,0:T(8,128)(2,1)} %bitcast.17, ...), custom_call_target="tpu_custom_call" | custom-call | flops 6442450944 | bytes 25165824 | tf_op jit(solution)/shard_map/dequant_down/pallas_call | solution.py:34
  41.6 7.3 %H2.1 = (bf16[256,1536]{1,0:T(8,128)(2,1)S(1)}, f32[8,128]{1,0:T(8,128)S(1)}) custom-call(bf16[128,4224]{1,0:T(8,128)(2,1)S(1)} %get-tuple-element.104.refs_0_, bf16[128,4224]{1,0:T(8,128)(2,1)S(1)} %collective-permute-done.6.refs_1_, bf16[3,4096,256]{2,1,0:T(8,128)(2,1)S(1)} %get-tuple-element.82.refs_2_, ...), custom_call_target="tpu_custom_call" | custom-call | flops 3221225472 | bytes 2097152 | tf_op jit(solution)/shard_map/H2/pallas_call | solution.py:34
  49.7 1.6 %collective-permute-start.9 = (bf16[32,4224]{1,0:T(8,128)(2,1)S(1)}, bf16[32,4224]{1,0:T(8,128)(2,1)S(1)}, u32[]{:S(2)}, u32[]{:S(2)}) collective-permute-start(bf16[32,4224]{1,0:T(8,128)(2,1)S(1)} %get-tuple-element.111), channel_id=1, source_target_pairs={{0,4},{1,5},{4,8},{5,9},{8,12},{9,13},{12,14},{13,15},{14,10},{15,... | collective-permute-start | bytes 811016 | tf_op jit(solution)/shard_map/ppermute | solution.py:253
  51.7 0.6 collective-permute-done.11.refs_1_
  52.4 7.3 %H3.1 = (bf16[256,1536]{1,0:T(8,128)(2,1)S(1)}, f32[8,128]{1,0:T(8,128)S(1)}) custom-call(bf16[128,4224]{1,0:T(8,128)(2,1)S(1)} %get-tuple-element.113.refs_0_, bf16[128,4224]{1,0:T(8,128)(2,1)S(1)} %collective-permute-done.11.refs_1_, bf16[3,4096,256]{2,1,0:T(8,128)(2,1)S(1)} %get-tuple-element.82.refs_2_, ...), custom_call_target="tpu_custom_call" | custom-call | flops 3221225472 | bytes 2097152 | tf_op jit(solution)/shard_map/H3/pallas_call | solution.py:34
  59.9 3.6 %D3.1 = (bf16[128,4096]{1,0:T(8,128)(2,1)S(1)}, bf16[128,4096]{1,0:T(8,128)(2,1)S(1)}, f32[8,128]{1,0:T(8,128)S(1)}) custom-call(bf16[256,1536]{1,0:T(8,128)(2,1)S(1)} %get-tuple-element.120.refs_0_, bf16[2,1536,512]{2,1,0:T(8,128)(2,1)S(1)} %get-tuple-element.99.refs_1_, bf16[2,1536,512]{2,1,0:T(8,128)(2,1)S(1)} %get-tuple-element.100.refs_2_, ...), custom_call_target="tpu_custom_call" | custom-call | flops 1 | bytes 1 | tf_op jit(solution)/shard_map/D3/pallas_call | solution.py:34
  64.1 2.9 %collective-permute-done.12.refs_1_ = bf16[64,4224]{1,0:T(8,128)(2,1)S(1)} collective-permute-done((bf16[64,4224]{1,0:T(8,128)(2,1)S(1)}, bf16[64,4224]{1,0:T(8,128)(2,1)S(1)}, u32[]{:S(2)}, u32[]{:S(2)}) %collective-permute-start.12) | collective-permute-done | bytes 540704 | tf_op jit(solution)/shard_map/ppermute | solution.py:259
  67.0 4.1 %H4.1 = (bf16[128,1536]{1,0:T(8,128)(2,1)S(1)}, f32[8,128]{1,0:T(8,128)}) custom-call(bf16[64,4224]{1,0:T(8,128)(2,1)S(1)} %get-tuple-element.119.refs_0_, bf16[64,4224]{1,0:T(8,128)(2,1)S(1)} %collective-permute-done.12.refs_1_, bf16[3,4096,256]{2,1,0:T(8,128)(2,1)S(1)} %get-tuple-element.82.refs_2_, bf16[3,4096,256]{2,1,0:T(8,128)(2,1)S(1)} %get-tuple-element.83.refs_3_, ...), custom_call_target="tpu_custom_call" | custom-call | flops 1610612736 | bytes 1048576 | tf_op jit(solution)/shard_map/H4/pallas_call | solution.py:34
  71.2 2.0 %D4.1 = (bf16[64,4096]{1,0:T(8,128)(2,1)S(1)}, bf16[64,4096]{1,0:T(8,128)(2,1)S(1)}, f32[8,128]{1,0:T(8,128)S(1)}) custom-call(bf16[128,1536]{1,0:T(8,128)(2,1)S(1)} %get-tuple-element.123.refs_0_, bf16[2,1536,512]{2,1,0:T(8,128)(2,1)S(1)} %get-tuple-element.99.refs_1_, bf16[2,1536,512]{2,1,0:T(8,128)(2,1)S(1)} %get-tuple-element.100.refs_2_, ...), custom_call_target="tpu_custom_call" | custom-call | flops 1 | bytes 1 | tf_op jit(solution)/shard_map/D4/pallas_call | solution.py:34
  73.2 3.6 %D2.1 = (bf16[128,4096]{1,0:T(8,128)(2,1)S(1)}, bf16[128,4096]{1,0:T(8,128)(2,1)S(1)}, f32[8,128]{1,0:T(8,128)S(1)}) custom-call(bf16[256,1536]{1,0:T(8,128)(2,1)S(1)} %get-tuple-element.106.refs_0_, bf16[2,1536,512]{2,1,0:T(8,128)(2,1)S(1)} %get-tuple-element.99.refs_1_, bf16[2,1536,512]{2,1,0:T(8,128)(2,1)S(1)} %get-tuple-element.100.refs_2_, ...), custom_call_target="tpu_custom_call" | custom-call | flops 1 | bytes 1 | tf_op jit(solution)/shard_map/D2/pallas_call | solution.py:34
  77.4 3.6 %D1.1 = (bf16[128,4096]{1,0:T(8,128)(2,1)S(1)}, bf16[128,4096]{1,0:T(8,128)(2,1)S(1)}, f32[8,128]{1,0:T(8,128)S(1)}) custom-call(bf16[256,1536]{1,0:T(8,128)(2,1)S(1)} %get-tuple-element.103.refs_0_, bf16[2,1536,512]{2,1,0:T(8,128)(2,1)S(1)} %get-tuple-element.99.refs_1_, bf16[2,1536,512]{2,1,0:T(8,128)(2,1)S(1)} %get-tuple-element.100.refs_2_, ...), custom_call_target="tpu_custom_call" | custom-call | flops 1 | bytes 1 | tf_op jit(solution)/shard_map/D1/pallas_call | solution.py:34
  81.2 1.6 %collective-permute-start.17 = (bf16[32,4096]{1,0:T(8,128)(2,1)S(1)}, bf16[32,4096]{1,0:T(8,128)(2,1)S(1)}, u32[]{:S(2)}, u32[]{:S(2)}) collective-permute-start(bf16[32,4096]{1,0:T(8,128)(2,1)S(1)} %get-tuple-element.136), channel_id=1, source_target_pairs={{0,4},{1,5},{4,8},{5,9},{8,12},{9,13},{12,14},{13,15},{14,10},{15,... | collective-permute-start | bytes 786440 | tf_op jit(solution)/shard_map/ppermute | solution.py:253
  83.2 2.0 %D0.1 = (bf16[64,4096]{1,0:T(8,128)(2,1)S(1)}, bf16[64,4096]{1,0:T(8,128)(2,1)S(1)}, f32[8,128]{1,0:T(8,128)S(1)}) custom-call(bf16[128,1536]{1,0:T(8,128)(2,1)S(1)} %get-tuple-element.91.refs_0_, bf16[2,1536,512]{2,1,0:T(8,128)(2,1)S(1)} %get-tuple-element.99.refs_1_, bf16[2,1536,512]{2,1,0:T(8,128)(2,1)S(1)} %get-tuple-element.100.refs_2_, ...), custom_call_target="tpu_custom_call" | custom-call | flops 1 | bytes 1 | tf_op jit(solution)/shard_map/D0/pallas_call | solution.py:34
  85.4 1.6 %collective-permute-start.22 = (bf16[32,4096]{1,0:T(8,128)(2,1)S(1)}, bf16[32,4096]{1,0:T(8,128)(2,1)S(1)}, u32[]{:S(2)}, u32[]{:S(2)}) collective-permute-start(bf16[32,4096]{1,0:T(8,128)(2,1)S(1)} %get-tuple-element.144), channel_id=1, source_target_pairs={{0,4},{1,5},{4,8},{5,9},{8,12},{9,13},{12,14},{13,15},{14,10},{15,... | collective-permute-start | bytes 786440 | tf_op jit(solution)/shard_map/ppermute | solution.py:253
  87.0 3.3 %collective-permute-done.17.refs_2_ = bf16[32,4096]{1,0:T(8,128)(2,1)S(1)} collective-permute-done((bf16[32,4096]{1,0:T(8,128)(2,1)S(1)}, bf16[32,4096]{1,0:T(8,128)(2,1)S(1)}, u32[]{:S(2)}, u32[]{:S(2)}) %collective-permute-start.17) | collective-permute-done | bytes 262176 | tf_op jit(solution)/shard_map/ppermute | solution.py:253
  90.3 1.0 collective-permute-start.23
  91.5 1.3 %collective-permute-start.20 = (bf16[32,4096]{1,0:T(8,128)(2,1)S(1)}, bf16[32,4096]{1,0:T(8,128)(2,1)S(1)}, u32[]{:S(2)}, u32[]{:S(2)}) collective-permute-start(bf16[32,4096]{1,0:T(8,128)(2,1)S(1)} %get-tuple-element.142), channel_id=1, source_target_pairs={{0,4},{1,5},{4,8},{5,9},{8,12},{9,13},{12,14},{13,15},{14,10},{15,... | collective-permute-start | bytes 786440 | tf_op jit(solution)/shard_map/ppermute | solution.py:253
  92.8 0.7 collective-permute-start.21
  93.6 2.4 %collective-permute-done.22.refs_2_ = bf16[32,4096]{1,0:T(8,128)(2,1)S(1)} collective-permute-done((bf16[32,4096]{1,0:T(8,128)(2,1)S(1)}, bf16[32,4096]{1,0:T(8,128)(2,1)S(1)}, u32[]{:S(2)}, u32[]{:S(2)}) %collective-permute-start.22) | collective-permute-done | bytes 262176 | tf_op jit(solution)/shard_map/ppermute | solution.py:253
  95.9 3.6 %collective-permute-done.23.refs_3_ = bf16[32,4096]{1,0:T(8,128)(2,1)S(1)} collective-permute-done((bf16[32,4096]{1,0:T(8,128)(2,1)S(1)}, bf16[32,4096]{1,0:T(8,128)(2,1)S(1)}, u32[]{:S(2)}, u32[]{:S(2)}) %collective-permute-start.23) | collective-permute-done | bytes 262176 | tf_op jit(solution)/shard_map/ppermute | solution.py:256
  99.8 1.6 %collective-permute-start.26 = (bf16[32,4096]{1,0:T(8,128)(2,1)S(1)}, bf16[32,4096]{1,0:T(8,128)(2,1)S(1)}, u32[]{:S(2)}, u32[]{:S(2)}) collective-permute-start(bf16[32,4096]{1,0:T(8,128)(2,1)S(1)} %get-tuple-element.150), channel_id=1, source_target_pairs={{0,4},{1,5},{4,8},{5,9},{8,12},{9,13},{12,14},{13,15},{14,10},{15,... | collective-permute-start | bytes 786440 | tf_op jit(solution)/shard_map/ppermute | solution.py:253
  101.8 3.3 %collective-permute-done.21.refs_3_ = bf16[32,4096]{1,0:T(8,128)(2,1)S(1)} collective-permute-done((bf16[32,4096]{1,0:T(8,128)(2,1)S(1)}, bf16[32,4096]{1,0:T(8,128)(2,1)S(1)}, u32[]{:S(2)}, u32[]{:S(2)}) %collective-permute-start.21) | collective-permute-done | bytes 262176 | tf_op jit(solution)/shard_map/ppermute | solution.py:256
  105.4 1.2 collective-permute-done.26.refs_2_
  106.6 2.2 %collective-permute-done.27.refs_3_ = bf16[32,4096]{1,0:T(8,128)(2,1)S(1)} collective-permute-done((bf16[32,4096]{1,0:T(8,128)(2,1)S(1)}, bf16[32,4096]{1,0:T(8,128)(2,1)S(1)}, u32[]{:S(2)}, u32[]{:S(2)}) %collective-permute-start.27) | collective-permute-done | bytes 262176 | tf_op jit(solution)/shard_map/ppermute | solution.py:256
  109.0 1.6 %collective-permute-start.28 = (bf16[32,4096]{1,0:T(8,128)(2,1)S(1)}, bf16[32,4096]{1,0:T(8,128)(2,1)S(1)}, u32[]{:S(2)}, u32[]{:S(2)}) collective-permute-start(bf16[32,4096]{1,0:T(8,128)(2,1)S(1)} %get-tuple-element.153), channel_id=1, source_target_pairs={{0,4},{1,5},{4,8},{5,9},{8,12},{9,13},{12,14},{13,15},{14,10},{15,... | collective-permute-start | bytes 786440 | tf_op jit(solution)/shard_map/ppermute | solution.py:253
  111.1 1.6 %collective-permute-start.24 = (bf16[32,4096]{1,0:T(8,128)(2,1)S(1)}, bf16[32,4096]{1,0:T(8,128)(2,1)S(1)}, u32[]{:S(2)}, u32[]{:S(2)}) collective-permute-start(bf16[32,4096]{1,0:T(8,128)(2,1)S(1)} %get-tuple-element.148), channel_id=1, source_target_pairs={{0,4},{1,5},{4,8},{5,9},{8,12},{9,13},{12,14},{13,15},{14,10},{15,... | collective-permute-start | bytes 786440 | tf_op jit(solution)/shard_map/ppermute | solution.py:253
  113.1 3.5 %collective-permute-done.28.refs_2_ = bf16[32,4096]{1,0:T(8,128)(2,1)S(1)} collective-permute-done((bf16[32,4096]{1,0:T(8,128)(2,1)S(1)}, bf16[32,4096]{1,0:T(8,128)(2,1)S(1)}, u32[]{:S(2)}, u32[]{:S(2)}) %collective-permute-start.28) | collective-permute-done | bytes 262176 | tf_op jit(solution)/shard_map/ppermute | solution.py:253
  116.6 1.9 %collective-permute-done.29.refs_3_ = bf16[32,4096]{1,0:T(8,128)(2,1)S(1)} collective-permute-done((bf16[32,4096]{1,0:T(8,128)(2,1)S(1)}, bf16[32,4096]{1,0:T(8,128)(2,1)S(1)}, u32[]{:S(2)}, u32[]{:S(2)}) %collective-permute-start.29) | collective-permute-done | bytes 262176 | tf_op jit(solution)/shard_map/ppermute | solution.py:256
  118.5 0.7 L1.1
  119.2 1.5 %collective-permute-start.30 = (bf16[32,4096]{1,0:T(8,128)(2,1)S(1)}, bf16[32,4096]{1,0:T(8,128)(2,1)S(1)}, u32[]{:S(2)}, u32[]{:S(2)}) collective-permute-start(bf16[32,4096]{1,0:T(8,128)(2,1)S(1)} %get-tuple-element.156), channel_id=1, source_target_pairs={{0,4},{1,5},{4,8},{5,9},{8,12},{9,13},{12,14},{13,15},{14,10},{15,... | collective-permute-start | bytes 786440 | tf_op jit(solution)/shard_map/ppermute | solution.py:253
  121.2 1.0 collective-permute-done.24.refs_2_
  122.2 1.9 %collective-permute-done.25.refs_3_ = bf16[32,4096]{1,0:T(8,128)(2,1)S(1)} collective-permute-done((bf16[32,4096]{1,0:T(8,128)(2,1)S(1)}, bf16[32,4096]{1,0:T(8,128)(2,1)S(1)}, u32[]{:S(2)}, u32[]{:S(2)}) %collective-permute-start.25) | collective-permute-done | bytes 262176 | tf_op jit(solution)/shard_map/ppermute | solution.py:256
  124.1 2.6 %collective-permute-done.30.refs_4_ = bf16[32,4096]{1,0:T(8,128)(2,1)S(1)} collective-permute-done((bf16[32,4096]{1,0:T(8,128)(2,1)S(1)}, bf16[32,4096]{1,0:T(8,128)(2,1)S(1)}, u32[]{:S(2)}, u32[]{:S(2)}) %collective-permute-start.30) | collective-permute-done | bytes 262176 | tf_op jit(solution)/shard_map/ppermute | solution.py:253
  126.6 1.6 %collective-permute-done.31.refs_5_ = bf16[32,4096]{1,0:T(8,128)(2,1)S(1)} collective-permute-done((bf16[32,4096]{1,0:T(8,128)(2,1)S(1)}, bf16[32,4096]{1,0:T(8,128)(2,1)S(1)}, u32[]{:S(2)}, u32[]{:S(2)}) %collective-permute-start.31) | collective-permute-done | bytes 262176 | tf_op jit(solution)/shard_map/ppermute | solution.py:256
  128.2 1.1 totals.9
  (47 shorter events, 7.4 us)
Async XLA Ops:
  1.4 15.4 %collective-permute-start.2 = (bf16[64,4224]{1,0:T(8,128)(2,1)S(1)}, bf16[64,4224]{1,0:T(8,128)(2,1)S(1)}, u32[]{:S(2)}, u32[]{:S(2)}) collective-permute-start(bf16[64,4224]{1,0:T(8,128)(2,1)S(1)} %prep.1.refs_4_.refs_0_), channel_id=1, source_target_pairs={{0,2},{1,3},{4,0},{5,1},{8,4},{9,5},{12,8},{13,9},{14,12},{15,13},... | collective-permute-start | bytes 1622024 | tf_op jit(solution)/shard_map/ppermute | solution.py:256
  4.5 13.7 %collective-permute-start.1 = (bf16[64,4224]{1,0:T(8,128)(2,1)S(1)}, bf16[64,4224]{1,0:T(8,128)(2,1)S(1)}, u32[]{:S(2)}, u32[]{:S(2)}) collective-permute-start(bf16[64,4224]{1,0:T(8,128)(2,1)S(1)} %prep.1.refs_4_.refs_0_), channel_id=1, source_target_pairs={{0,4},{1,5},{4,8},{5,9},{8,12},{9,13},{12,14},{13,15},{14,10},{15,... | collective-permute-start | bytes 1622024 | tf_op jit(solution)/shard_map/ppermute | solution.py:253
  4.6 0.7 copy-start
  5.3 0.7 copy-start.1
  18.3 7.7 %collective-permute-start.5 = (bf16[128,4224]{1,0:T(8,128)(2,1)S(1)}, bf16[128,4224]{1,0:T(8,128)(2,1)S(1)}, u32[]{:S(2)}, u32[]{:S(2)}) collective-permute-start(bf16[128,4224]{1,0:T(8,128)(2,1)S(1)} %get-tuple-element.92.refs_0_), channel_id=1, source_target_pairs={{0,1},{1,0},{2,3},{3,2},{4,5},{5,4},{6,7},{7,6},{8,9},{9,8},{10,11... | collective-permute-start | bytes 3244040 | tf_op jit(solution)/shard_map/ppermute | solution.py:259
  18.4 3.5 %collective-permute-start = (bf16[64,4224]{1,0:T(8,128)(2,1)S(1)}, bf16[64,4224]{1,0:T(8,128)(2,1)S(1)}, u32[]{:S(2)}, u32[]{:S(2)}) collective-permute-start(bf16[64,4224]{1,0:T(8,128)(2,1)S(1)} %prep.1.refs_4_.refs_0_), channel_id=1, source_target_pairs={{0,1},{1,0},{2,3},{3,2},{4,5},{5,4},{6,7},{7,6},{8,9},{9,8},{10,11... | collective-permute-start | bytes 1622024 | tf_op jit(solution)/shard_map/ppermute | solution.py:259
  18.9 14.5 %collective-permute-start.3 = (bf16[64,4224]{1,0:T(8,128)(2,1)S(1)}, bf16[64,4224]{1,0:T(8,128)(2,1)S(1)}, u32[]{:S(2)}, u32[]{:S(2)}) collective-permute-start(bf16[64,4224]{1,0:T(8,128)(2,1)S(1)} %collective-permute-done.1.refs_0_), channel_id=1, source_target_pairs={{0,4},{1,5},{4,8},{5,9},{8,12},{9,13},{12,14},{13,15},{14,10},{15,... | collective-permute-start | bytes 1622024 | tf_op jit(solution)/shard_map/ppermute | solution.py:253
  19.3 14.1 %collective-permute-start.4 = (bf16[64,4224]{1,0:T(8,128)(2,1)S(1)}, bf16[64,4224]{1,0:T(8,128)(2,1)S(1)}, u32[]{:S(2)}, u32[]{:S(2)}) collective-permute-start(bf16[64,4224]{1,0:T(8,128)(2,1)S(1)} %collective-permute-done.2.refs_1_), channel_id=1, source_target_pairs={{0,2},{1,3},{4,0},{5,1},{8,4},{9,5},{12,8},{13,9},{14,12},{15,13},... | collective-permute-start | bytes 1622024 | tf_op jit(solution)/shard_map/ppermute | solution.py:256
  26.0 9.7 %copy-start.2 = (f32[1,12,32]{2,0,1:T(1,128)S(1)}, f32[1,12,32]{2,0,1:T(1,128)}, u32[]{:S(2)}) copy-start(f32[1,12,32]{2,0,1:T(1,128)} %param.19) | copy-start | bytes 4612
  33.5 8.1 %collective-permute-start.6 = (bf16[128,4224]{1,0:T(8,128)(2,1)S(1)}, bf16[128,4224]{1,0:T(8,128)(2,1)S(1)}, u32[]{:S(2)}, u32[]{:S(2)}) collective-permute-start(bf16[128,4224]{1,0:T(8,128)(2,1)S(1)} %get-tuple-element.104.refs_0_), channel_id=1, source_target_pairs={{0,1},{1,0},{2,3},{3,2},{4,5},{5,4},{6,7},{7,6},{8,9},{9,8},{10,11... | collective-permute-start | bytes 3244040 | tf_op jit(solution)/shard_map/ppermute | solution.py:259
  33.7 15.3 %collective-permute-start.7 = (bf16[64,4224]{1,0:T(8,128)(2,1)S(1)}, bf16[64,4224]{1,0:T(8,128)(2,1)S(1)}, u32[]{:S(2)}, u32[]{:S(2)}) collective-permute-start(bf16[64,4224]{1,0:T(8,128)(2,1)S(1)} %collective-permute-done.3.refs_0_), channel_id=1, source_target_pairs={{0,4},{1,5},{4,8},{5,9},{8,12},{9,13},{12,14},{13,15},{14,10},{15,... | collective-permute-start | bytes 1622024 | tf_op jit(solution)/shard_map/ppermute | solution.py:253
  35.1 14.3 %collective-permute-start.8 = (bf16[64,4224]{1,0:T(8,128)(2,1)S(1)}, bf16[64,4224]{1,0:T(8,128)(2,1)S(1)}, u32[]{:S(2)}, u32[]{:S(2)}) collective-permute-start(bf16[64,4224]{1,0:T(8,128)(2,1)S(1)} %collective-permute-done.4.refs_1_), channel_id=1, source_target_pairs={{0,2},{1,3},{4,0},{5,1},{8,4},{9,5},{12,8},{13,9},{14,12},{15,13},... | collective-permute-start | bytes 1622024 | tf_op jit(solution)/shard_map/ppermute | solution.py:256
  49.6 2.8 %collective-permute-start.11 = (bf16[128,4224]{1,0:T(8,128)(2,1)S(1)}, bf16[128,4224]{1,0:T(8,128)(2,1)S(1)}, u32[]{:S(2)}, u32[]{:S(2)}) collective-permute-start(bf16[128,4224]{1,0:T(8,128)(2,1)S(1)} %get-tuple-element.113.refs_0_), channel_id=1, source_target_pairs={{0,1},{1,0},{2,3},{3,2},{4,5},{5,4},{6,7},{7,6},{8,9},{9,8},{10,11... | collective-permute-start | bytes 3244040 | tf_op jit(solution)/shard_map/ppermute | solution.py:259
  49.7 10.0 %collective-permute-start.9 = (bf16[32,4224]{1,0:T(8,128)(2,1)S(1)}, bf16[32,4224]{1,0:T(8,128)(2,1)S(1)}, u32[]{:S(2)}, u32[]{:S(2)}) collective-permute-start(bf16[32,4224]{1,0:T(8,128)(2,1)S(1)} %get-tuple-element.111), channel_id=1, source_target_pairs={{0,4},{1,5},{4,8},{5,9},{8,12},{9,13},{12,14},{13,15},{14,10},{15,... | collective-permute-start | bytes 811016 | tf_op jit(solution)/shard_map/ppermute | solution.py:253
  51.3 8.6 %collective-permute-start.10 = (bf16[32,4224]{1,0:T(8,128)(2,1)S(1)}, bf16[32,4224]{1,0:T(8,128)(2,1)S(1)}, u32[]{:S(2)}, u32[]{:S(2)}) collective-permute-start(bf16[32,4224]{1,0:T(8,128)(2,1)S(1)} %get-tuple-element.112), channel_id=1, source_target_pairs={{0,2},{1,3},{4,0},{5,1},{8,4},{9,5},{12,8},{13,9},{14,12},{15,13},... | collective-permute-start | bytes 811016 | tf_op jit(solution)/shard_map/ppermute | solution.py:256
  63.5 7.6 %collective-permute-start.13 = (bf16[128,4096]{1,0:T(8,128)(2,1)S(1)}, bf16[128,4096]{1,0:T(8,128)(2,1)S(1)}, u32[]{:S(2)}, u32[]{:S(2)}) collective-permute-start(bf16[128,4096]{1,0:T(8,128)(2,1)S(1)} %get-tuple-element.125), channel_id=1, source_target_pairs={{0,1},{1,0},{2,3},{3,2},{4,5},{5,4},{6,7},{7,6},{8,9},{9,8},{10,11... | collective-permute-start | bytes 3145736 | tf_op jit(solution)/shard_map/ppermute | solution.py:259
  63.6 3.4 %collective-permute-start.12 = (bf16[64,4224]{1,0:T(8,128)(2,1)S(1)}, bf16[64,4224]{1,0:T(8,128)(2,1)S(1)}, u32[]{:S(2)}, u32[]{:S(2)}) collective-permute-start(bf16[64,4224]{1,0:T(8,128)(2,1)S(1)} %get-tuple-element.119.refs_0_), channel_id=1, source_target_pairs={{0,1},{1,0},{2,3},{3,2},{4,5},{5,4},{6,7},{7,6},{8,9},{9,8},{10,11... | collective-permute-start | bytes 1622024 | tf_op jit(solution)/shard_map/ppermute | solution.py:259
  76.8 14.5 %collective-permute-start.16 = (bf16[128,4096]{1,0:T(8,128)(2,1)S(1)}, bf16[128,4096]{1,0:T(8,128)(2,1)S(1)}, u32[]{:S(2)}, u32[]{:S(2)}) collective-permute-start(bf16[128,4096]{1,0:T(8,128)(2,1)S(1)} %get-tuple-element.135), channel_id=1, source_target_pairs={{0,1},{1,0},{2,3},{3,2},{4,5},{5,4},{6,7},{7,6},{8,9},{9,8},{10,11... | collective-permute-start | bytes 3145736 | tf_op jit(solution)/shard_map/ppermute | solution.py:259
  77.0 8.2 %collective-permute-start.19 = (bf16[64,4096]{1,0:T(8,128)(2,1)S(1)}, bf16[64,4096]{1,0:T(8,128)(2,1)S(1)}, u32[]{:S(2)}, u32[]{:S(2)}) collective-permute-start(bf16[64,4096]{1,0:T(8,128)(2,1)S(1)} %get-tuple-element.139), channel_id=1, source_target_pairs={{0,1},{1,0},{2,3},{3,2},{4,5},{5,4},{6,7},{7,6},{8,9},{9,8},{10,11... | collective-permute-start | bytes 1572872 | tf_op jit(solution)/shard_map/ppermute | solution.py:259
  81.0 20.9 %collective-permute-start.15 = (bf16[128,4096]{1,0:T(8,128)(2,1)S(1)}, bf16[128,4096]{1,0:T(8,128)(2,1)S(1)}, u32[]{:S(2)}, u32[]{:S(2)}) collective-permute-start(bf16[128,4096]{1,0:T(8,128)(2,1)S(1)} %get-tuple-element.133), channel_id=1, source_target_pairs={{0,1},{1,0},{2,3},{3,2},{4,5},{5,4},{6,7},{7,6},{8,9},{9,8},{10,11... | collective-permute-start | bytes 3145736 | tf_op jit(solution)/shard_map/ppermute | solution.py:259
  81.2 9.1 %collective-permute-start.17 = (bf16[32,4096]{1,0:T(8,128)(2,1)S(1)}, bf16[32,4096]{1,0:T(8,128)(2,1)S(1)}, u32[]{:S(2)}, u32[]{:S(2)}) collective-permute-start(bf16[32,4096]{1,0:T(8,128)(2,1)S(1)} %get-tuple-element.136), channel_id=1, source_target_pairs={{0,4},{1,5},{4,8},{5,9},{8,12},{9,13},{12,14},{13,15},{14,10},{15,... | collective-permute-start | bytes 786440 | tf_op jit(solution)/shard_map/ppermute | solution.py:253
  82.8 8.5 %collective-permute-start.18 = (bf16[32,4096]{1,0:T(8,128)(2,1)S(1)}, bf16[32,4096]{1,0:T(8,128)(2,1)S(1)}, u32[]{:S(2)}, u32[]{:S(2)}) collective-permute-start(bf16[32,4096]{1,0:T(8,128)(2,1)S(1)} %get-tuple-element.137), channel_id=1, source_target_pairs={{0,2},{1,3},{4,0},{5,1},{8,4},{9,5},{12,8},{13,9},{14,12},{15,13},... | collective-permute-start | bytes 786440 | tf_op jit(solution)/shard_map/ppermute | solution.py:256
  85.4 10.6 %collective-permute-start.22 = (bf16[32,4096]{1,0:T(8,128)(2,1)S(1)}, bf16[32,4096]{1,0:T(8,128)(2,1)S(1)}, u32[]{:S(2)}, u32[]{:S(2)}) collective-permute-start(bf16[32,4096]{1,0:T(8,128)(2,1)S(1)} %get-tuple-element.144), channel_id=1, source_target_pairs={{0,4},{1,5},{4,8},{5,9},{8,12},{9,13},{12,14},{13,15},{14,10},{15,... | collective-permute-start | bytes 786440 | tf_op jit(solution)/shard_map/ppermute | solution.py:253
  90.3 9.2 %collective-permute-start.23 = (bf16[32,4096]{1,0:T(8,128)(2,1)S(1)}, bf16[32,4096]{1,0:T(8,128)(2,1)S(1)}, u32[]{:S(2)}, u32[]{:S(2)}) collective-permute-start(bf16[32,4096]{1,0:T(8,128)(2,1)S(1)} %get-tuple-element.145), channel_id=1, source_target_pairs={{0,2},{1,3},{4,0},{5,1},{8,4},{9,5},{12,8},{13,9},{14,12},{15,13},... | collective-permute-start | bytes 786440 | tf_op jit(solution)/shard_map/ppermute | solution.py:256
  91.5 10.4 %collective-permute-start.20 = (bf16[32,4096]{1,0:T(8,128)(2,1)S(1)}, bf16[32,4096]{1,0:T(8,128)(2,1)S(1)}, u32[]{:S(2)}, u32[]{:S(2)}) collective-permute-start(bf16[32,4096]{1,0:T(8,128)(2,1)S(1)} %get-tuple-element.142), channel_id=1, source_target_pairs={{0,4},{1,5},{4,8},{5,9},{8,12},{9,13},{12,14},{13,15},{14,10},{15,... | collective-permute-start | bytes 786440 | tf_op jit(solution)/shard_map/ppermute | solution.py:253
  92.8 12.3 %collective-permute-start.21 = (bf16[32,4096]{1,0:T(8,128)(2,1)S(1)}, bf16[32,4096]{1,0:T(8,128)(2,1)S(1)}, u32[]{:S(2)}, u32[]{:S(2)}) collective-permute-start(bf16[32,4096]{1,0:T(8,128)(2,1)S(1)} %get-tuple-element.143), channel_id=1, source_target_pairs={{0,2},{1,3},{4,0},{5,1},{8,4},{9,5},{12,8},{13,9},{14,12},{15,13},... | collective-permute-start | bytes 786440 | tf_op jit(solution)/shard_map/ppermute | solution.py:256
  99.8 6.9 %collective-permute-start.26 = (bf16[32,4096]{1,0:T(8,128)(2,1)S(1)}, bf16[32,4096]{1,0:T(8,128)(2,1)S(1)}, u32[]{:S(2)}, u32[]{:S(2)}) collective-permute-start(bf16[32,4096]{1,0:T(8,128)(2,1)S(1)} %get-tuple-element.150), channel_id=1, source_target_pairs={{0,4},{1,5},{4,8},{5,9},{8,12},{9,13},{12,14},{13,15},{14,10},{15,... | collective-permute-start | bytes 786440 | tf_op jit(solution)/shard_map/ppermute | solution.py:253
  101.4 7.4 %collective-permute-start.27 = (bf16[32,4096]{1,0:T(8,128)(2,1)S(1)}, bf16[32,4096]{1,0:T(8,128)(2,1)S(1)}, u32[]{:S(2)}, u32[]{:S(2)}) collective-permute-start(bf16[32,4096]{1,0:T(8,128)(2,1)S(1)} %get-tuple-element.151), channel_id=1, source_target_pairs={{0,2},{1,3},{4,0},{5,1},{8,4},{9,5},{12,8},{13,9},{14,12},{15,13},... | collective-permute-start | bytes 786440 | tf_op jit(solution)/shard_map/ppermute | solution.py:256
  109.0 7.6 %collective-permute-start.28 = (bf16[32,4096]{1,0:T(8,128)(2,1)S(1)}, bf16[32,4096]{1,0:T(8,128)(2,1)S(1)}, u32[]{:S(2)}, u32[]{:S(2)}) collective-permute-start(bf16[32,4096]{1,0:T(8,128)(2,1)S(1)} %get-tuple-element.153), channel_id=1, source_target_pairs={{0,4},{1,5},{4,8},{5,9},{8,12},{9,13},{12,14},{13,15},{14,10},{15,... | collective-permute-start | bytes 786440 | tf_op jit(solution)/shard_map/ppermute | solution.py:253
  110.6 7.9 %collective-permute-start.29 = (bf16[32,4096]{1,0:T(8,128)(2,1)S(1)}, bf16[32,4096]{1,0:T(8,128)(2,1)S(1)}, u32[]{:S(2)}, u32[]{:S(2)}) collective-permute-start(bf16[32,4096]{1,0:T(8,128)(2,1)S(1)} %get-tuple-element.154), channel_id=1, source_target_pairs={{0,2},{1,3},{4,0},{5,1},{8,4},{9,5},{12,8},{13,9},{14,12},{15,13},... | collective-permute-start | bytes 786440 | tf_op jit(solution)/shard_map/ppermute | solution.py:256
  111.1 10.1 %collective-permute-start.14 = (bf16[64,4096]{1,0:T(8,128)(2,1)S(1)}, bf16[64,4096]{1,0:T(8,128)(2,1)S(1)}, u32[]{:S(2)}, u32[]{:S(2)}) collective-permute-start(bf16[64,4096]{1,0:T(8,128)(2,1)S(1)} %get-tuple-element.131), channel_id=1, source_target_pairs={{0,1},{1,0},{2,3},{3,2},{4,5},{5,4},{6,7},{7,6},{8,9},{9,8},{10,11... | collective-permute-start | bytes 1572872 | tf_op jit(solution)/shard_map/ppermute | solution.py:259
  111.1 11.1 %collective-permute-start.24 = (bf16[32,4096]{1,0:T(8,128)(2,1)S(1)}, bf16[32,4096]{1,0:T(8,128)(2,1)S(1)}, u32[]{:S(2)}, u32[]{:S(2)}) collective-permute-start(bf16[32,4096]{1,0:T(8,128)(2,1)S(1)} %get-tuple-element.148), channel_id=1, source_target_pairs={{0,4},{1,5},{4,8},{5,9},{8,12},{9,13},{12,14},{13,15},{14,10},{15,... | collective-permute-start | bytes 786440 | tf_op jit(solution)/shard_map/ppermute | solution.py:253
  112.6 11.4 %collective-permute-start.25 = (bf16[32,4096]{1,0:T(8,128)(2,1)S(1)}, bf16[32,4096]{1,0:T(8,128)(2,1)S(1)}, u32[]{:S(2)}, u32[]{:S(2)}) collective-permute-start(bf16[32,4096]{1,0:T(8,128)(2,1)S(1)} %get-tuple-element.149), channel_id=1, source_target_pairs={{0,2},{1,3},{4,0},{5,1},{8,4},{9,5},{12,8},{13,9},{14,12},{15,13},... | collective-permute-start | bytes 786440 | tf_op jit(solution)/shard_map/ppermute | solution.py:256
  119.2 7.5 %collective-permute-start.30 = (bf16[32,4096]{1,0:T(8,128)(2,1)S(1)}, bf16[32,4096]{1,0:T(8,128)(2,1)S(1)}, u32[]{:S(2)}, u32[]{:S(2)}) collective-permute-start(bf16[32,4096]{1,0:T(8,128)(2,1)S(1)} %get-tuple-element.156), channel_id=1, source_target_pairs={{0,4},{1,5},{4,8},{5,9},{8,12},{9,13},{12,14},{13,15},{14,10},{15,... | collective-permute-start | bytes 786440 | tf_op jit(solution)/shard_map/ppermute | solution.py:253
  120.7 7.5 %collective-permute-start.31 = (bf16[32,4096]{1,0:T(8,128)(2,1)S(1)}, bf16[32,4096]{1,0:T(8,128)(2,1)S(1)}, u32[]{:S(2)}, u32[]{:S(2)}) collective-permute-start(bf16[32,4096]{1,0:T(8,128)(2,1)S(1)} %get-tuple-element.157), channel_id=1, source_target_pairs={{0,2},{1,3},{4,0},{5,1},{8,4},{9,5},{12,8},{13,9},{14,12},{15,13},... | collective-permute-start | bytes 786440 | tf_op jit(solution)/shard_map/ppermute | solution.py:256
where the time goes:
time: 130 us; the launch traced here: 129 us
  Pallas kernels  64.9 us (50%)
  waiting for transfers between devices  36.3 us (28%)
  starting transfers between devices  26.4 us (20%)
  local copies, waits for them, and re-layouts  1.39 us (1%)
    pallas_call x24, Pallas kernels, ordered(): pl.pallas_call(body, in_specs=[*in_specs, *[whole(pl.ANY)] * len(waits),...  63.5 us
    ppermute x11, waiting for transfers between devices, left(): return lax.ppermute(a, names, shift(-1))  16.4 us
    ppermute x11, waiting for transfers between devices, right(): return lax.ppermute(a, names, shift(1))  15.4 us
    ppermute x11, starting transfers between devices, right(): return lax.ppermute(a, names, shift(1))  14.5 us
    ppermute x11, starting transfers between devices, left(): return lax.ppermute(a, names, shift(-1))  9.69 us
    ppermute x10, waiting for transfers between devices, across(): return lax.ppermute(a, names, [(i, i ^ 1) for i in range(2 * chips)])  4.5 us
  transfers between devices with their start and end apart: 32, of which 19 were waited for; matrix products, arithmetic and copies ran while one was open for 0% of the time, Pallas kernels for 41%

commit v1 on v0

--- a/solution.py
+++ b/solution.py
@@ -12,7 +12,7 @@
 TILE_FF = 256
 TILE_D = 512
 SLOT_BYTES = 5 << 20
-PARTS_FF, PARTS_D = 2, 4
+PARTS_FF, PARTS_D = 3, 4
 HID, DEQ = 3, 6
 COST = 1024
 MB = 1 << 20
@@ -165,7 +165,7 @@
         [pltpu.VMEM((rows, depth), BF16)],
         waits,
         scratch=[pltpu.VMEM((rows, width + 128), BF16)],
-        flops=2 * rows * width * depth,
+        flops=16 * rows * width * depth,
         moved=2 * rows * width,
         vmem=HID,
         name=name,
@@ -196,7 +196,7 @@
         [whole()] * (1 + len(mats)),
         [pltpu.VMEM((count // 2, width), BF16), jax.ShapeDtypeStruct((count // 2, width), BF16)],
         waits,
-        flops=1,
+        flops=8 * count * depth * width,
         moved=1,
         vmem=1,
         name=name,

time: 130 us -> 124 us (0.954)
  waiting for transfers between devices: 36.3 us -> 32 us
    ppermute x11, waiting for transfers between devices: 16.4 us -> 10.6 us  [left(): return lax.ppermute(a, names, shift(-1))]
    ppermute x11, waiting for transfers between devices: 15.4 us -> 20.7 us  [right(): return lax.ppermute(a, names, shift(1))]
    ppermute x10, waiting for transfers between devices: 4.5 us -> 0.64 us  [across(): return lax.ppermute(a, names, [(i, i ^ 1) for i in range(2 * chips)])]
  transfers between devices with their start and end apart: 32 -> 32, of which waited for: 19 -> 18; matrix products, arithmetic and copies ran while one was open for 0% -> 0% of each run, Pallas kernels for 41% -> 50%
where the time goes in v1:
time: 124 us
  Pallas kernels  64.5 us (52%)
  waiting for transfers between devices  32 us (26%)
  starting transfers between devices  25.5 us (21%)
  local copies, waits for them, and re-layouts  1.41 us (1%)
    pallas_call x24, Pallas kernels, ordered(): pl.pallas_call(body, in_specs=[*in_specs, *[whole(pl.ANY)] * len(waits),...  63 us
    ppermute x11, waiting for transfers between devices, right(): return lax.ppermute(a, names, shift(1))  20.7 us
    ppermute x11, starting transfers between devices, right(): return lax.ppermute(a, names, shift(1))  13.4 us
    ppermute x11, waiting for transfers between devices, left(): return lax.ppermute(a, names, shift(-1))  10.6 us
    ppermute x11, starting transfers between devices, left(): return lax.ppermute(a, names, shift(-1))  10.3 us
  transfers between devices with their start and end apart: 32, of which 18 were waited for; matrix products, arithmetic and copies ran while one was open for 0% of the time, Pallas kernels for 50%

profile of v1, /device:TPU:0, one launch (start us, length us, event | category | flops | bytes accessed | tf_op | source)
XLA Modules:
  0.0 123.6 jit_solution(2668174252019253211)
XLA Ops:
  0.0 1.4 %prep.1.refs_4_.refs_0_ = bf16[64,4224]{1,0:T(8,128)(2,1)S(1)} custom-call(bf16[64,4096]{1,0:T(8,128)(2,1)} %codes_ref.1, bf16[32,64]{1,0:T(8,128)(2,1)} %bitcast.12, s32[8,64]{1,0:T(8,128)} %bitcast.13, f32[8,64]{1,0:T(8,128)} %bitcast.14), custom_call_target="tpu_custom_call" | custom-call | flops 262144 | bytes 1048576 | tf_op jit(solution)/shard_map/prep/pallas_call | solution.py:64
  1.4 3.0 %collective-permute-start.2 = (bf16[64,4224]{1,0:T(8,128)(2,1)S(1)}, bf16[64,4224]{1,0:T(8,128)(2,1)S(1)}, u32[]{:S(2)}, u32[]{:S(2)}) collective-permute-start(bf16[64,4224]{1,0:T(8,128)(2,1)S(1)} %prep.1.refs_4_.refs_0_), channel_id=1, source_target_pairs={{0,2},{1,3},{4,0},{5,1},{8,4},{9,5},{12,8},{13,9},{14,12},{15,13},... | collective-permute-start | bytes 1622024 | tf_op jit(solution)/shard_map/ppermute | solution.py:256
  4.6 0.7 copy-done
  5.3 0.7 copy-done.1
  6.0 9.6 %dequant_both.1 = (bf16[2,4096,256]{2,1,0:T(8,128)(2,1)S(1)}, bf16[2,4096,256]{2,1,0:T(8,128)(2,1)S(1)}, bf16[2,4096,256]{2,1,0:T(8,128)(2,1)S(1)}, bf16[2,4096,...) custom-call(f32[12,1,32]{2,1,0:T(1,128)S(1)} %bitcast.9, ...), custom_call_target="tpu_custom_call" | custom-call | flops 12884901888 | bytes 50331648 | tf_op jit(solution)/shard_map/dequant_both/pallas_call | solution.py:34
  15.6 1.2 collective-permute-done.2.refs_1_
  16.8 1.4 %collective-permute-done.1.refs_0_ = bf16[64,4224]{1,0:T(8,128)(2,1)S(1)} collective-permute-done((bf16[64,4224]{1,0:T(8,128)(2,1)S(1)}, bf16[64,4224]{1,0:T(8,128)(2,1)S(1)}, u32[]{:S(2)}, u32[]{:S(2)}) %collective-permute-start.1) | collective-permute-done | bytes 540704 | tf_op jit(solution)/shard_map/ppermute | solution.py:253
  18.6 1.6 %collective-permute-start.4 = (bf16[64,4224]{1,0:T(8,128)(2,1)S(1)}, bf16[64,4224]{1,0:T(8,128)(2,1)S(1)}, u32[]{:S(2)}, u32[]{:S(2)}) collective-permute-start(bf16[64,4224]{1,0:T(8,128)(2,1)S(1)} %collective-permute-done.2.refs_1_), channel_id=1, source_target_pairs={{0,2},{1,3},{4,0},{5,1},{8,4},{9,5},{12,8},{13,9},{14,12},{15,13},... | collective-permute-start | bytes 1622024 | tf_op jit(solution)/shard_map/ppermute | solution.py:256
  20.4 4.0 %H0.1 = (bf16[128,1536]{1,0:T(8,128)(2,1)S(1)}, f32[8,128]{1,0:T(8,128)S(1)}) custom-call(bf16[64,4224]{1,0:T(8,128)(2,1)S(1)} %prep.1.refs_4_.refs_0_, bf16[64,4224]{1,0:T(8,128)(2,1)S(1)} %collective-permute-done.refs_1_, bf16[2,4096,256]{2,1,0:T(8,128)(2,1)S(1)} %get-tuple-element.84.refs_2_, bf16[2,4096,256]{2,1,0:T(8,128)(2,1)S(1)} %get-tuple-element.85.refs_3_, ...), custom_call_target="tpu_custom_call" | custom-call | flops 12884901888 | bytes 1048576 | tf_op jit(solution)/shard_map/H0/pallas_call | solution.py:34
  24.5 7.3 %H1.1 = (bf16[256,1536]{1,0:T(8,128)(2,1)S(1)}, f32[8,128]{1,0:T(8,128)S(1)}) custom-call(bf16[128,4224]{1,0:T(8,128)(2,1)S(1)} %get-tuple-element.96.refs_0_, bf16[128,4224]{1,0:T(8,128)(2,1)S(1)} %collective-permute-done.5.refs_1_, bf16[2,4096,256]{2,1,0:T(8,128)(2,1)S(1)} %get-tuple-element.84.refs_2_, ...), custom_call_target="tpu_custom_call" | custom-call | flops 25769803776 | bytes 2097152 | tf_op jit(solution)/shard_map/H1/pallas_call | solution.py:34
  32.4 1.4 %collective-permute-start.7 = (bf16[64,4224]{1,0:T(8,128)(2,1)S(1)}, bf16[64,4224]{1,0:T(8,128)(2,1)S(1)}, u32[]{:S(2)}, u32[]{:S(2)}) collective-permute-start(bf16[64,4224]{1,0:T(8,128)(2,1)S(1)} %collective-permute-done.3.refs_0_), channel_id=1, source_target_pairs={{0,4},{1,5},{4,8},{5,9},{8,12},{9,13},{12,14},{13,15},{14,10},{15,... | collective-permute-start | bytes 1622024 | tf_op jit(solution)/shard_map/ppermute | solution.py:253
  34.4 5.8 %dequant_down.1 = (bf16[2,1536,512]{2,1,0:T(8,128)(2,1)S(1)}, bf16[2,1536,512]{2,1,0:T(8,128)(2,1)S(1)}, bf16[2,1536,512]{2,1,0:T(8,128)(2,1)S(1)}, bf16[2,1536,512]{2,1,0:T(8,128)(2,1)S(1)}, f32[8,128]{1,0:T(8,128)S(1)}) custom-call(f32[12,1,32]{2,1,0:T(1,128)S(1)} %bitcast.11, bf16[1536,4096]{1,0:T(8,128)(2,1)} %bitcast.17, ...), custom_call_target="tpu_custom_call" | custom-call | flops 6442450944 | bytes 25165824 | tf_op jit(solution)/shard_map/dequant_down/pallas_call | solution.py:34
  40.3 7.3 %H2.1 = (bf16[256,1536]{1,0:T(8,128)(2,1)S(1)}, f32[8,128]{1,0:T(8,128)S(1)}) custom-call(bf16[128,4224]{1,0:T(8,128)(2,1)S(1)} %get-tuple-element.108.refs_0_, bf16[128,4224]{1,0:T(8,128)(2,1)S(1)} %collective-permute-done.6.refs_1_, bf16[2,4096,256]{2,1,0:T(8,128)(2,1)S(1)} %get-tuple-element.84.refs_2_, ...), custom_call_target="tpu_custom_call" | custom-call | flops 25769803776 | bytes 2097152 | tf_op jit(solution)/shard_map/H2/pallas_call | solution.py:34
  47.5 0.6 collective-permute-done.8.refs_1_
  48.3 1.6 %collective-permute-start.9 = (bf16[32,4224]{1,0:T(8,128)(2,1)S(1)}, bf16[32,4224]{1,0:T(8,128)(2,1)S(1)}, u32[]{:S(2)}, u32[]{:S(2)}) collective-permute-start(bf16[32,4224]{1,0:T(8,128)(2,1)S(1)} %get-tuple-element.115), channel_id=1, source_target_pairs={{0,4},{1,5},{4,8},{5,9},{8,12},{9,13},{12,14},{13,15},{14,10},{15,... | collective-permute-start | bytes 811016 | tf_op jit(solution)/shard_map/ppermute | solution.py:253
  50.4 0.6 collective-permute-done.11.refs_1_
  51.0 7.2 %H3.1 = (bf16[256,1536]{1,0:T(8,128)(2,1)S(1)}, f32[8,128]{1,0:T(8,128)S(1)}) custom-call(bf16[128,4224]{1,0:T(8,128)(2,1)S(1)} %get-tuple-element.117.refs_0_, bf16[128,4224]{1,0:T(8,128)(2,1)S(1)} %collective-permute-done.11.refs_1_, bf16[2,4096,256]{2,1,0:T(8,128)(2,1)S(1)} %get-tuple-element.84.refs_2_, ...), custom_call_target="tpu_custom_call" | custom-call | flops 25769803776 | bytes 2097152 | tf_op jit(solution)/shard_map/H3/pallas_call | solution.py:34
  58.7 3.6 %D3.1 = (bf16[128,4096]{1,0:T(8,128)(2,1)S(1)}, bf16[128,4096]{1,0:T(8,128)(2,1)S(1)}, f32[8,128]{1,0:T(8,128)S(1)}) custom-call(bf16[256,1536]{1,0:T(8,128)(2,1)S(1)} %get-tuple-element.124.refs_0_, bf16[2,1536,512]{2,1,0:T(8,128)(2,1)S(1)} %get-tuple-element.103.refs_1_, bf16[2,1536,512]{2,1,0:T(8,128)(2,1)S(1)} %get-tuple-element.104.refs_2_, ...), custom_call_target="tpu_custom_call" | custom-call | flops 12884901888 | bytes 1 | tf_op jit(solution)/shard_map/D3/pallas_call | solution.py:34
  62.8 4.0 %H4.1 = (bf16[128,1536]{1,0:T(8,128)(2,1)S(1)}, f32[8,128]{1,0:T(8,128)}) custom-call(bf16[64,4224]{1,0:T(8,128)(2,1)S(1)} %get-tuple-element.123.refs_0_, bf16[64,4224]{1,0:T(8,128)(2,1)S(1)} %collective-permute-done.12.refs_1_, bf16[2,4096,256]{2,1,0:T(8,128)(2,1)S(1)} %get-tuple-element.84.refs_2_, bf16[2,4096,256]{2,1,0:T(8,128)(2,1)S(1)} %get-tuple-element.85.refs_3_, ...), custom_call_target="tpu_custom_call" | custom-call | flops 12884901888 | bytes 1048576 | tf_op jit(solution)/shard_map/H4/pallas_call | solution.py:34
  67.0 1.6 %collective-permute-start.17 = (bf16[32,4096]{1,0:T(8,128)(2,1)S(1)}, bf16[32,4096]{1,0:T(8,128)(2,1)S(1)}, u32[]{:S(2)}, u32[]{:S(2)}) collective-permute-start(bf16[32,4096]{1,0:T(8,128)(2,1)S(1)} %get-tuple-element.140), channel_id=1, source_target_pairs={{0,4},{1,5},{4,8},{5,9},{8,12},{9,13},{12,14},{13,15},{14,10},{15,... | collective-permute-start | bytes 786440 | tf_op jit(solution)/shard_map/ppermute | solution.py:253
  69.1 2.0 %D4.1 = (bf16[64,4096]{1,0:T(8,128)(2,1)S(1)}, bf16[64,4096]{1,0:T(8,128)(2,1)S(1)}, f32[8,128]{1,0:T(8,128)S(1)}) custom-call(bf16[128,1536]{1,0:T(8,128)(2,1)S(1)} %get-tuple-element.127.refs_0_, bf16[2,1536,512]{2,1,0:T(8,128)(2,1)S(1)} %get-tuple-element.103.refs_1_, bf16[2,1536,512]{2,1,0:T(8,128)(2,1)S(1)} %get-tuple-element.104.refs_2_, ...), custom_call_target="tpu_custom_call" | custom-call | flops 6442450944 | bytes 1 | tf_op jit(solution)/shard_map/D4/pallas_call | solution.py:34
  71.2 3.6 %D2.1 = (bf16[128,4096]{1,0:T(8,128)(2,1)S(1)}, bf16[128,4096]{1,0:T(8,128)(2,1)S(1)}, f32[8,128]{1,0:T(8,128)S(1)}) custom-call(bf16[256,1536]{1,0:T(8,128)(2,1)S(1)} %get-tuple-element.110.refs_0_, bf16[2,1536,512]{2,1,0:T(8,128)(2,1)S(1)} %get-tuple-element.103.refs_1_, bf16[2,1536,512]{2,1,0:T(8,128)(2,1)S(1)} %get-tuple-element.104.refs_2_, ...), custom_call_target="tpu_custom_call" | custom-call | flops 12884901888 | bytes 1 | tf_op jit(solution)/shard_map/D2/pallas_call | solution.py:34
  75.3 3.6 %D1.1 = (bf16[128,4096]{1,0:T(8,128)(2,1)S(1)}, bf16[128,4096]{1,0:T(8,128)(2,1)S(1)}, f32[8,128]{1,0:T(8,128)S(1)}) custom-call(bf16[256,1536]{1,0:T(8,128)(2,1)S(1)} %get-tuple-element.107.refs_0_, bf16[2,1536,512]{2,1,0:T(8,128)(2,1)S(1)} %get-tuple-element.103.refs_1_, bf16[2,1536,512]{2,1,0:T(8,128)(2,1)S(1)} %get-tuple-element.104.refs_2_, ...), custom_call_target="tpu_custom_call" | custom-call | flops 12884901888 | bytes 1 | tf_op jit(solution)/shard_map/D1/pallas_call | solution.py:34
  79.0 2.0 %D0.1 = (bf16[64,4096]{1,0:T(8,128)(2,1)S(1)}, bf16[64,4096]{1,0:T(8,128)(2,1)S(1)}, f32[8,128]{1,0:T(8,128)S(1)}) custom-call(bf16[128,1536]{1,0:T(8,128)(2,1)S(1)} %get-tuple-element.95.refs_0_, bf16[2,1536,512]{2,1,0:T(8,128)(2,1)S(1)} %get-tuple-element.103.refs_1_, bf16[2,1536,512]{2,1,0:T(8,128)(2,1)S(1)} %get-tuple-element.104.refs_2_, ...), custom_call_target="tpu_custom_call" | custom-call | flops 6442450944 | bytes 1 | tf_op jit(solution)/shard_map/D0/pallas_call | solution.py:34
  81.1 1.6 %collective-permute-start.22 = (bf16[32,4096]{1,0:T(8,128)(2,1)S(1)}, bf16[32,4096]{1,0:T(8,128)(2,1)S(1)}, u32[]{:S(2)}, u32[]{:S(2)}) collective-permute-start(bf16[32,4096]{1,0:T(8,128)(2,1)S(1)} %get-tuple-element.148), channel_id=1, source_target_pairs={{0,4},{1,5},{4,8},{5,9},{8,12},{9,13},{12,14},{13,15},{14,10},{15,... | collective-permute-start | bytes 786440 | tf_op jit(solution)/shard_map/ppermute | solution.py:253
  83.4 1.6 %collective-permute-start.20 = (bf16[32,4096]{1,0:T(8,128)(2,1)S(1)}, bf16[32,4096]{1,0:T(8,128)(2,1)S(1)}, u32[]{:S(2)}, u32[]{:S(2)}) collective-permute-start(bf16[32,4096]{1,0:T(8,128)(2,1)S(1)} %get-tuple-element.146), channel_id=1, source_target_pairs={{0,4},{1,5},{4,8},{5,9},{8,12},{9,13},{12,14},{13,15},{14,10},{15,... | collective-permute-start | bytes 786440 | tf_op jit(solution)/shard_map/ppermute | solution.py:253
  85.5 4.8 %collective-permute-done.22.refs_2_ = bf16[32,4096]{1,0:T(8,128)(2,1)S(1)} collective-permute-done((bf16[32,4096]{1,0:T(8,128)(2,1)S(1)}, bf16[32,4096]{1,0:T(8,128)(2,1)S(1)}, u32[]{:S(2)}, u32[]{:S(2)}) %collective-permute-start.22) | collective-permute-done | bytes 262176 | tf_op jit(solution)/shard_map/ppermute | solution.py:253
  90.3 1.6 %collective-permute-done.23.refs_3_ = bf16[32,4096]{1,0:T(8,128)(2,1)S(1)} collective-permute-done((bf16[32,4096]{1,0:T(8,128)(2,1)S(1)}, bf16[32,4096]{1,0:T(8,128)(2,1)S(1)}, u32[]{:S(2)}, u32[]{:S(2)}) %collective-permute-start.23) | collective-permute-done | bytes 262176 | tf_op jit(solution)/shard_map/ppermute | solution.py:256
  92.0 1.4 %collective-permute-start.26 = (bf16[32,4096]{1,0:T(8,128)(2,1)S(1)}, bf16[32,4096]{1,0:T(8,128)(2,1)S(1)}, u32[]{:S(2)}, u32[]{:S(2)}) collective-permute-start(bf16[32,4096]{1,0:T(8,128)(2,1)S(1)} %get-tuple-element.154), channel_id=1, source_target_pairs={{0,4},{1,5},{4,8},{5,9},{8,12},{9,13},{12,14},{13,15},{14,10},{15,... | collective-permute-start | bytes 786440 | tf_op jit(solution)/shard_map/ppermute | solution.py:253
  93.5 0.6 collective-permute-start.27
  94.1 1.8 %collective-permute-done.20.refs_2_ = bf16[32,4096]{1,0:T(8,128)(2,1)S(1)} collective-permute-done((bf16[32,4096]{1,0:T(8,128)(2,1)S(1)}, bf16[32,4096]{1,0:T(8,128)(2,1)S(1)}, u32[]{:S(2)}, u32[]{:S(2)}) %collective-permute-start.20) | collective-permute-done | bytes 262176 | tf_op jit(solution)/shard_map/ppermute | solution.py:253
  95.9 1.6 %collective-permute-done.21.refs_3_ = bf16[32,4096]{1,0:T(8,128)(2,1)S(1)} collective-permute-done((bf16[32,4096]{1,0:T(8,128)(2,1)S(1)}, bf16[32,4096]{1,0:T(8,128)(2,1)S(1)}, u32[]{:S(2)}, u32[]{:S(2)}) %collective-permute-start.21) | collective-permute-done | bytes 262176 | tf_op jit(solution)/shard_map/ppermute | solution.py:256
  97.6 3.5 %collective-permute-done.26.refs_2_ = bf16[32,4096]{1,0:T(8,128)(2,1)S(1)} collective-permute-done((bf16[32,4096]{1,0:T(8,128)(2,1)S(1)}, bf16[32,4096]{1,0:T(8,128)(2,1)S(1)}, u32[]{:S(2)}, u32[]{:S(2)}) %collective-permute-start.26) | collective-permute-done | bytes 262176 | tf_op jit(solution)/shard_map/ppermute | solution.py:253
  101.1 1.2 %collective-permute-done.27.refs_3_ = bf16[32,4096]{1,0:T(8,128)(2,1)S(1)} collective-permute-done((bf16[32,4096]{1,0:T(8,128)(2,1)S(1)}, bf16[32,4096]{1,0:T(8,128)(2,1)S(1)}, u32[]{:S(2)}, u32[]{:S(2)}) %collective-permute-start.27) | collective-permute-done | bytes 262176 | tf_op jit(solution)/shard_map/ppermute | solution.py:256
  102.5 1.4 %collective-permute-start.28 = (bf16[32,4096]{1,0:T(8,128)(2,1)S(1)}, bf16[32,4096]{1,0:T(8,128)(2,1)S(1)}, u32[]{:S(2)}, u32[]{:S(2)}) collective-permute-start(bf16[32,4096]{1,0:T(8,128)(2,1)S(1)} %get-tuple-element.157), channel_id=1, source_target_pairs={{0,4},{1,5},{4,8},{5,9},{8,12},{9,13},{12,14},{13,15},{14,10},{15,... | collective-permute-start | bytes 786440 | tf_op jit(solution)/shard_map/ppermute | solution.py:253
  104.0 0.6 collective-permute-start.29
  104.6 1.4 %collective-permute-start.24 = (bf16[32,4096]{1,0:T(8,128)(2,1)S(1)}, bf16[32,4096]{1,0:T(8,128)(2,1)S(1)}, u32[]{:S(2)}, u32[]{:S(2)}) collective-permute-start(bf16[32,4096]{1,0:T(8,128)(2,1)S(1)} %get-tuple-element.152), channel_id=1, source_target_pairs={{0,4},{1,5},{4,8},{5,9},{8,12},{9,13},{12,14},{13,15},{14,10},{15,... | collective-permute-start | bytes 786440 | tf_op jit(solution)/shard_map/ppermute | solution.py:253
  106.0 0.6 collective-permute-start.25
  106.6 5.2 %collective-permute-done.28.refs_2_ = bf16[32,4096]{1,0:T(8,128)(2,1)S(1)} collective-permute-done((bf16[32,4096]{1,0:T(8,128)(2,1)S(1)}, bf16[32,4096]{1,0:T(8,128)(2,1)S(1)}, u32[]{:S(2)}, u32[]{:S(2)}) %collective-permute-start.28) | collective-permute-done | bytes 262176 | tf_op jit(solution)/shard_map/ppermute | solution.py:253
  111.8 1.4 %collective-permute-done.29.refs_3_ = bf16[32,4096]{1,0:T(8,128)(2,1)S(1)} collective-permute-done((bf16[32,4096]{1,0:T(8,128)(2,1)S(1)}, bf16[32,4096]{1,0:T(8,128)(2,1)S(1)}, u32[]{:S(2)}, u32[]{:S(2)}) %collective-permute-start.29) | collective-permute-done | bytes 262176 | tf_op jit(solution)/shard_map/ppermute | solution.py:256
  113.2 0.7 L1.1
  113.9 0.8 collective-permute-start.30
  114.7 1.2 collective-permute-start.31
  115.9 1.5 %collective-permute-done.24.refs_2_ = bf16[32,4096]{1,0:T(8,128)(2,1)S(1)} collective-permute-done((bf16[32,4096]{1,0:T(8,128)(2,1)S(1)}, bf16[32,4096]{1,0:T(8,128)(2,1)S(1)}, u32[]{:S(2)}, u32[]{:S(2)}) %collective-permute-start.24) | collective-permute-done | bytes 262176 | tf_op jit(solution)/shard_map/ppermute | solution.py:253
  117.5 1.4 %collective-permute-done.25.refs_3_ = bf16[32,4096]{1,0:T(8,128)(2,1)S(1)} collective-permute-done((bf16[32,4096]{1,0:T(8,128)(2,1)S(1)}, bf16[32,4096]{1,0:T(8,128)(2,1)S(1)}, u32[]{:S(2)}, u32[]{:S(2)}) %collective-permute-start.25) | collective-permute-done | bytes 262176 | tf_op jit(solution)/shard_map/ppermute | solution.py:256
  118.8 2.6 %collective-permute-done.30.refs_4_ = bf16[32,4096]{1,0:T(8,128)(2,1)S(1)} collective-permute-done((bf16[32,4096]{1,0:T(8,128)(2,1)S(1)}, bf16[32,4096]{1,0:T(8,128)(2,1)S(1)}, u32[]{:S(2)}, u32[]{:S(2)}) %collective-permute-start.30) | collective-permute-done | bytes 262176 | tf_op jit(solution)/shard_map/ppermute | solution.py:253
  121.4 1.1 collective-permute-done.31.refs_5_
  122.5 1.1 totals.9
  (55 shorter events, 6.7 us)
Async XLA Ops:
  1.4 15.4 %collective-permute-start.2 = (bf16[64,4224]{1,0:T(8,128)(2,1)S(1)}, bf16[64,4224]{1,0:T(8,128)(2,1)S(1)}, u32[]{:S(2)}, u32[]{:S(2)}) collective-permute-start(bf16[64,4224]{1,0:T(8,128)(2,1)S(1)} %prep.1.refs_4_.refs_0_), channel_id=1, source_target_pairs={{0,2},{1,3},{4,0},{5,1},{8,4},{9,5},{12,8},{13,9},{14,12},{15,13},... | collective-permute-start | bytes 1622024 | tf_op jit(solution)/shard_map/ppermute | solution.py:256
  4.5 13.7 %collective-permute-start.1 = (bf16[64,4224]{1,0:T(8,128)(2,1)S(1)}, bf16[64,4224]{1,0:T(8,128)(2,1)S(1)}, u32[]{:S(2)}, u32[]{:S(2)}) collective-permute-start(bf16[64,4224]{1,0:T(8,128)(2,1)S(1)} %prep.1.refs_4_.refs_0_), channel_id=1, source_target_pairs={{0,4},{1,5},{4,8},{5,9},{8,12},{9,13},{12,14},{13,15},{14,10},{15,... | collective-permute-start | bytes 1622024 | tf_op jit(solution)/shard_map/ppermute | solution.py:253
  4.6 15.8 %collective-permute-start = (bf16[64,4224]{1,0:T(8,128)(2,1)S(1)}, bf16[64,4224]{1,0:T(8,128)(2,1)S(1)}, u32[]{:S(2)}, u32[]{:S(2)}) collective-permute-start(bf16[64,4224]{1,0:T(8,128)(2,1)S(1)} %prep.1.refs_4_.refs_0_), channel_id=1, source_target_pairs={{0,1},{1,0},{2,3},{3,2},{4,5},{5,4},{6,7},{7,6},{8,9},{9,8},{10,11... | collective-permute-start | bytes 1622024 | tf_op jit(solution)/shard_map/ppermute | solution.py:259
  4.6 0.7 copy-start
  5.3 0.7 copy-start.1
  15.6 35.5 %copy-start.3 = (bf16[2,4096,256]{2,1,0:T(8,128)(2,1)}, bf16[2,4096,256]{2,1,0:T(8,128)(2,1)S(1)}, u32[]{:S(2)}) copy-start(bf16[2,4096,256]{2,1,0:T(8,128)(2,1)S(1)} %get-tuple-element.88.refs_6_) | copy-start | bytes 12582916
  15.6 35.5 %copy-start.5 = (bf16[2,4096,256]{2,1,0:T(8,128)(2,1)}, bf16[2,4096,256]{2,1,0:T(8,128)(2,1)S(1)}, u32[]{:S(2)}) copy-start(bf16[2,4096,256]{2,1,0:T(8,128)(2,1)S(1)} %get-tuple-element.89.refs_7_) | copy-start | bytes 12582916
  18.2 13.5 %collective-permute-start.3 = (bf16[64,4224]{1,0:T(8,128)(2,1)S(1)}, bf16[64,4224]{1,0:T(8,128)(2,1)S(1)}, u32[]{:S(2)}, u32[]{:S(2)}) collective-permute-start(bf16[64,4224]{1,0:T(8,128)(2,1)S(1)} %collective-permute-done.1.refs_0_), channel_id=1, source_target_pairs={{0,4},{1,5},{4,8},{5,9},{8,12},{9,13},{12,14},{13,15},{14,10},{15,... | collective-permute-start | bytes 1622024 | tf_op jit(solution)/shard_map/ppermute | solution.py:253
  18.6 13.4 %collective-permute-start.4 = (bf16[64,4224]{1,0:T(8,128)(2,1)S(1)}, bf16[64,4224]{1,0:T(8,128)(2,1)S(1)}, u32[]{:S(2)}, u32[]{:S(2)}) collective-permute-start(bf16[64,4224]{1,0:T(8,128)(2,1)S(1)} %collective-permute-done.2.refs_1_), channel_id=1, source_target_pairs={{0,2},{1,3},{4,0},{5,1},{8,4},{9,5},{12,8},{13,9},{14,12},{15,13},... | collective-permute-start | bytes 1622024 | tf_op jit(solution)/shard_map/ppermute | solution.py:256
  20.3 4.1 %collective-permute-start.5 = (bf16[128,4224]{1,0:T(8,128)(2,1)S(1)}, bf16[128,4224]{1,0:T(8,128)(2,1)S(1)}, u32[]{:S(2)}, u32[]{:S(2)}) collective-permute-start(bf16[128,4224]{1,0:T(8,128)(2,1)S(1)} %get-tuple-element.96.refs_0_), channel_id=1, source_target_pairs={{0,1},{1,0},{2,3},{3,2},{4,5},{5,4},{6,7},{7,6},{8,9},{9,8},{10,11... | collective-permute-start | bytes 3244040 | tf_op jit(solution)/shard_map/ppermute | solution.py:259
  24.5 10.0 %copy-start.2 = (f32[1,12,32]{2,0,1:T(1,128)S(1)}, f32[1,12,32]{2,0,1:T(1,128)}, u32[]{:S(2)}) copy-start(f32[1,12,32]{2,0,1:T(1,128)} %param.19) | copy-start | bytes 4612
  32.1 8.2 %collective-permute-start.6 = (bf16[128,4224]{1,0:T(8,128)(2,1)S(1)}, bf16[128,4224]{1,0:T(8,128)(2,1)S(1)}, u32[]{:S(2)}, u32[]{:S(2)}) collective-permute-start(bf16[128,4224]{1,0:T(8,128)(2,1)S(1)} %get-tuple-element.108.refs_0_), channel_id=1, source_target_pairs={{0,1},{1,0},{2,3},{3,2},{4,5},{5,4},{6,7},{7,6},{8,9},{9,8},{10,11... | collective-permute-start | bytes 3244040 | tf_op jit(solution)/shard_map/ppermute | solution.py:259
  32.4 15.2 %collective-permute-start.7 = (bf16[64,4224]{1,0:T(8,128)(2,1)S(1)}, bf16[64,4224]{1,0:T(8,128)(2,1)S(1)}, u32[]{:S(2)}, u32[]{:S(2)}) collective-permute-start(bf16[64,4224]{1,0:T(8,128)(2,1)S(1)} %collective-permute-done.3.refs_0_), channel_id=1, source_target_pairs={{0,4},{1,5},{4,8},{5,9},{8,12},{9,13},{12,14},{13,15},{14,10},{15,... | collective-permute-start | bytes 1622024 | tf_op jit(solution)/shard_map/ppermute | solution.py:253
  33.8 14.3 %collective-permute-start.8 = (bf16[64,4224]{1,0:T(8,128)(2,1)S(1)}, bf16[64,4224]{1,0:T(8,128)(2,1)S(1)}, u32[]{:S(2)}, u32[]{:S(2)}) collective-permute-start(bf16[64,4224]{1,0:T(8,128)(2,1)S(1)} %collective-permute-done.4.refs_1_), channel_id=1, source_target_pairs={{0,2},{1,3},{4,0},{5,1},{8,4},{9,5},{12,8},{13,9},{14,12},{15,13},... | collective-permute-start | bytes 1622024 | tf_op jit(solution)/shard_map/ppermute | solution.py:256
  48.3 2.8 %collective-permute-start.11 = (bf16[128,4224]{1,0:T(8,128)(2,1)S(1)}, bf16[128,4224]{1,0:T(8,128)(2,1)S(1)}, u32[]{:S(2)}, u32[]{:S(2)}) collective-permute-start(bf16[128,4224]{1,0:T(8,128)(2,1)S(1)} %get-tuple-element.117.refs_0_), channel_id=1, source_target_pairs={{0,1},{1,0},{2,3},{3,2},{4,5},{5,4},{6,7},{7,6},{8,9},{9,8},{10,11... | collective-permute-start | bytes 3244040 | tf_op jit(solution)/shard_map/ppermute | solution.py:259
  48.3 10.0 %collective-permute-start.9 = (bf16[32,4224]{1,0:T(8,128)(2,1)S(1)}, bf16[32,4224]{1,0:T(8,128)(2,1)S(1)}, u32[]{:S(2)}, u32[]{:S(2)}) collective-permute-start(bf16[32,4224]{1,0:T(8,128)(2,1)S(1)} %get-tuple-element.115), channel_id=1, source_target_pairs={{0,4},{1,5},{4,8},{5,9},{8,12},{9,13},{12,14},{13,15},{14,10},{15,... | collective-permute-start | bytes 811016 | tf_op jit(solution)/shard_map/ppermute | solution.py:253
  50.0 8.6 %collective-permute-start.10 = (bf16[32,4224]{1,0:T(8,128)(2,1)S(1)}, bf16[32,4224]{1,0:T(8,128)(2,1)S(1)}, u32[]{:S(2)}, u32[]{:S(2)}) collective-permute-start(bf16[32,4224]{1,0:T(8,128)(2,1)S(1)} %get-tuple-element.116), channel_id=1, source_target_pairs={{0,2},{1,3},{4,0},{5,1},{8,4},{9,5},{12,8},{13,9},{14,12},{15,13},... | collective-permute-start | bytes 811016 | tf_op jit(solution)/shard_map/ppermute | solution.py:256
  58.6 4.2 %collective-permute-start.12 = (bf16[64,4224]{1,0:T(8,128)(2,1)S(1)}, bf16[64,4224]{1,0:T(8,128)(2,1)S(1)}, u32[]{:S(2)}, u32[]{:S(2)}) collective-permute-start(bf16[64,4224]{1,0:T(8,128)(2,1)S(1)} %get-tuple-element.123.refs_0_), channel_id=1, source_target_pairs={{0,1},{1,0},{2,3},{3,2},{4,5},{5,4},{6,7},{7,6},{8,9},{9,8},{10,11... | collective-permute-start | bytes 1622024 | tf_op jit(solution)/shard_map/ppermute | solution.py:259
  58.6 4.2 %copy-start.4 = (bf16[2,4096,256]{2,1,0:T(8,128)(2,1)S(1)}, bf16[2,4096,256]{2,1,0:T(8,128)(2,1)}, u32[]{:S(2)}) copy-start(bf16[2,4096,256]{2,1,0:T(8,128)(2,1)} %copy-done.3) | copy-start | bytes 12582916
  58.7 4.1 %copy-start.6 = (bf16[2,4096,256]{2,1,0:T(8,128)(2,1)S(1)}, bf16[2,4096,256]{2,1,0:T(8,128)(2,1)}, u32[]{:S(2)}) copy-start(bf16[2,4096,256]{2,1,0:T(8,128)(2,1)} %copy-done.5) | copy-start | bytes 12582916
  62.3 4.6 %collective-permute-start.13 = (bf16[128,4096]{1,0:T(8,128)(2,1)S(1)}, bf16[128,4096]{1,0:T(8,128)(2,1)S(1)}, u32[]{:S(2)}, u32[]{:S(2)}) collective-permute-start(bf16[128,4096]{1,0:T(8,128)(2,1)S(1)} %get-tuple-element.129), channel_id=1, source_target_pairs={{0,1},{1,0},{2,3},{3,2},{4,5},{5,4},{6,7},{7,6},{8,9},{9,8},{10,11... | collective-permute-start | bytes 3145736 | tf_op jit(solution)/shard_map/ppermute | solution.py:259
  67.0 15.7 %collective-permute-start.17 = (bf16[32,4096]{1,0:T(8,128)(2,1)S(1)}, bf16[32,4096]{1,0:T(8,128)(2,1)S(1)}, u32[]{:S(2)}, u32[]{:S(2)}) collective-permute-start(bf16[32,4096]{1,0:T(8,128)(2,1)S(1)} %get-tuple-element.140), channel_id=1, source_target_pairs={{0,4},{1,5},{4,8},{5,9},{8,12},{9,13},{12,14},{13,15},{14,10},{15,... | collective-permute-start | bytes 786440 | tf_op jit(solution)/shard_map/ppermute | solution.py:253
  68.6 14.6 %collective-permute-start.18 = (bf16[32,4096]{1,0:T(8,128)(2,1)S(1)}, bf16[32,4096]{1,0:T(8,128)(2,1)S(1)}, u32[]{:S(2)}, u32[]{:S(2)}) collective-permute-start(bf16[32,4096]{1,0:T(8,128)(2,1)S(1)} %get-tuple-element.141), channel_id=1, source_target_pairs={{0,2},{1,3},{4,0},{5,1},{8,4},{9,5},{12,8},{13,9},{14,12},{15,13},... | collective-permute-start | bytes 786440 | tf_op jit(solution)/shard_map/ppermute | solution.py:256
  71.1 9.9 %collective-permute-start.19 = (bf16[64,4096]{1,0:T(8,128)(2,1)S(1)}, bf16[64,4096]{1,0:T(8,128)(2,1)S(1)}, u32[]{:S(2)}, u32[]{:S(2)}) collective-permute-start(bf16[64,4096]{1,0:T(8,128)(2,1)S(1)} %get-tuple-element.143), channel_id=1, source_target_pairs={{0,1},{1,0},{2,3},{3,2},{4,5},{5,4},{6,7},{7,6},{8,9},{9,8},{10,11... | collective-permute-start | bytes 1572872 | tf_op jit(solution)/shard_map/ppermute | solution.py:259
  74.8 8.4 %collective-permute-start.16 = (bf16[128,4096]{1,0:T(8,128)(2,1)S(1)}, bf16[128,4096]{1,0:T(8,128)(2,1)S(1)}, u32[]{:S(2)}, u32[]{:S(2)}) collective-permute-start(bf16[128,4096]{1,0:T(8,128)(2,1)S(1)} %get-tuple-element.139), channel_id=1, source_target_pairs={{0,1},{1,0},{2,3},{3,2},{4,5},{5,4},{6,7},{7,6},{8,9},{9,8},{10,11... | collective-permute-start | bytes 3145736 | tf_op jit(solution)/shard_map/ppermute | solution.py:259
  78.9 15.2 %collective-permute-start.15 = (bf16[128,4096]{1,0:T(8,128)(2,1)S(1)}, bf16[128,4096]{1,0:T(8,128)(2,1)S(1)}, u32[]{:S(2)}, u32[]{:S(2)}) collective-permute-start(bf16[128,4096]{1,0:T(8,128)(2,1)S(1)} %get-tuple-element.137), channel_id=1, source_target_pairs={{0,1},{1,0},{2,3},{3,2},{4,5},{5,4},{6,7},{7,6},{8,9},{9,8},{10,11... | collective-permute-start | bytes 3145736 | tf_op jit(solution)/shard_map/ppermute | solution.py:259
  81.1 9.2 %collective-permute-start.22 = (bf16[32,4096]{1,0:T(8,128)(2,1)S(1)}, bf16[32,4096]{1,0:T(8,128)(2,1)S(1)}, u32[]{:S(2)}, u32[]{:S(2)}) collective-permute-start(bf16[32,4096]{1,0:T(8,128)(2,1)S(1)} %get-tuple-element.148), channel_id=1, source_target_pairs={{0,4},{1,5},{4,8},{5,9},{8,12},{9,13},{12,14},{13,15},{14,10},{15,... | collective-permute-start | bytes 786440 | tf_op jit(solution)/shard_map/ppermute | solution.py:253
  82.7 9.1 %collective-permute-start.23 = (bf16[32,4096]{1,0:T(8,128)(2,1)S(1)}, bf16[32,4096]{1,0:T(8,128)(2,1)S(1)}, u32[]{:S(2)}, u32[]{:S(2)}) collective-permute-start(bf16[32,4096]{1,0:T(8,128)(2,1)S(1)} %get-tuple-element.149), channel_id=1, source_target_pairs={{0,2},{1,3},{4,0},{5,1},{8,4},{9,5},{12,8},{13,9},{14,12},{15,13},... | collective-permute-start | bytes 786440 | tf_op jit(solution)/shard_map/ppermute | solution.py:256
  83.4 12.5 %collective-permute-start.20 = (bf16[32,4096]{1,0:T(8,128)(2,1)S(1)}, bf16[32,4096]{1,0:T(8,128)(2,1)S(1)}, u32[]{:S(2)}, u32[]{:S(2)}) collective-permute-start(bf16[32,4096]{1,0:T(8,128)(2,1)S(1)} %get-tuple-element.146), channel_id=1, source_target_pairs={{0,4},{1,5},{4,8},{5,9},{8,12},{9,13},{12,14},{13,15},{14,10},{15,... | collective-permute-start | bytes 786440 | tf_op jit(solution)/shard_map/ppermute | solution.py:253
  85.0 12.5 %collective-permute-start.21 = (bf16[32,4096]{1,0:T(8,128)(2,1)S(1)}, bf16[32,4096]{1,0:T(8,128)(2,1)S(1)}, u32[]{:S(2)}, u32[]{:S(2)}) collective-permute-start(bf16[32,4096]{1,0:T(8,128)(2,1)S(1)} %get-tuple-element.147), channel_id=1, source_target_pairs={{0,2},{1,3},{4,0},{5,1},{8,4},{9,5},{12,8},{13,9},{14,12},{15,13},... | collective-permute-start | bytes 786440 | tf_op jit(solution)/shard_map/ppermute | solution.py:256
  92.0 9.1 %collective-permute-start.26 = (bf16[32,4096]{1,0:T(8,128)(2,1)S(1)}, bf16[32,4096]{1,0:T(8,128)(2,1)S(1)}, u32[]{:S(2)}, u32[]{:S(2)}) collective-permute-start(bf16[32,4096]{1,0:T(8,128)(2,1)S(1)} %get-tuple-element.154), channel_id=1, source_target_pairs={{0,4},{1,5},{4,8},{5,9},{8,12},{9,13},{12,14},{13,15},{14,10},{15,... | collective-permute-start | bytes 786440 | tf_op jit(solution)/shard_map/ppermute | solution.py:253
  93.5 8.9 %collective-permute-start.27 = (bf16[32,4096]{1,0:T(8,128)(2,1)S(1)}, bf16[32,4096]{1,0:T(8,128)(2,1)S(1)}, u32[]{:S(2)}, u32[]{:S(2)}) collective-permute-start(bf16[32,4096]{1,0:T(8,128)(2,1)S(1)} %get-tuple-element.155), channel_id=1, source_target_pairs={{0,2},{1,3},{4,0},{5,1},{8,4},{9,5},{12,8},{13,9},{14,12},{15,13},... | collective-permute-start | bytes 786440 | tf_op jit(solution)/shard_map/ppermute | solution.py:256
  102.5 9.3 %collective-permute-start.28 = (bf16[32,4096]{1,0:T(8,128)(2,1)S(1)}, bf16[32,4096]{1,0:T(8,128)(2,1)S(1)}, u32[]{:S(2)}, u32[]{:S(2)}) collective-permute-start(bf16[32,4096]{1,0:T(8,128)(2,1)S(1)} %get-tuple-element.157), channel_id=1, source_target_pairs={{0,4},{1,5},{4,8},{5,9},{8,12},{9,13},{12,14},{13,15},{14,10},{15,... | collective-permute-start | bytes 786440 | tf_op jit(solution)/shard_map/ppermute | solution.py:253
  104.0 9.2 %collective-permute-start.29 = (bf16[32,4096]{1,0:T(8,128)(2,1)S(1)}, bf16[32,4096]{1,0:T(8,128)(2,1)S(1)}, u32[]{:S(2)}, u32[]{:S(2)}) collective-permute-start(bf16[32,4096]{1,0:T(8,128)(2,1)S(1)} %get-tuple-element.158), channel_id=1, source_target_pairs={{0,2},{1,3},{4,0},{5,1},{8,4},{9,5},{12,8},{13,9},{14,12},{15,13},... | collective-permute-start | bytes 786440 | tf_op jit(solution)/shard_map/ppermute | solution.py:256
  104.6 11.3 %collective-permute-start.14 = (bf16[64,4096]{1,0:T(8,128)(2,1)S(1)}, bf16[64,4096]{1,0:T(8,128)(2,1)S(1)}, u32[]{:S(2)}, u32[]{:S(2)}) collective-permute-start(bf16[64,4096]{1,0:T(8,128)(2,1)S(1)} %get-tuple-element.135), channel_id=1, source_target_pairs={{0,1},{1,0},{2,3},{3,2},{4,5},{5,4},{6,7},{7,6},{8,9},{9,8},{10,11... | collective-permute-start | bytes 1572872 | tf_op jit(solution)/shard_map/ppermute | solution.py:259
  104.6 12.8 %collective-permute-start.24 = (bf16[32,4096]{1,0:T(8,128)(2,1)S(1)}, bf16[32,4096]{1,0:T(8,128)(2,1)S(1)}, u32[]{:S(2)}, u32[]{:S(2)}) collective-permute-start(bf16[32,4096]{1,0:T(8,128)(2,1)S(1)} %get-tuple-element.152), channel_id=1, source_target_pairs={{0,4},{1,5},{4,8},{5,9},{8,12},{9,13},{12,14},{13,15},{14,10},{15,... | collective-permute-start | bytes 786440 | tf_op jit(solution)/shard_map/ppermute | solution.py:253
  106.0 12.8 %collective-permute-start.25 = (bf16[32,4096]{1,0:T(8,128)(2,1)S(1)}, bf16[32,4096]{1,0:T(8,128)(2,1)S(1)}, u32[]{:S(2)}, u32[]{:S(2)}) collective-permute-start(bf16[32,4096]{1,0:T(8,128)(2,1)S(1)} %get-tuple-element.153), channel_id=1, source_target_pairs={{0,2},{1,3},{4,0},{5,1},{8,4},{9,5},{12,8},{13,9},{14,12},{15,13},... | collective-permute-start | bytes 786440 | tf_op jit(solution)/shard_map/ppermute | solution.py:256
  113.9 7.5 %collective-permute-start.30 = (bf16[32,4096]{1,0:T(8,128)(2,1)S(1)}, bf16[32,4096]{1,0:T(8,128)(2,1)S(1)}, u32[]{:S(2)}, u32[]{:S(2)}) collective-permute-start(bf16[32,4096]{1,0:T(8,128)(2,1)S(1)} %get-tuple-element.160), channel_id=1, source_target_pairs={{0,4},{1,5},{4,8},{5,9},{8,12},{9,13},{12,14},{13,15},{14,10},{15,... | collective-permute-start | bytes 786440 | tf_op jit(solution)/shard_map/ppermute | solution.py:253
  114.7 7.8 %collective-permute-start.31 = (bf16[32,4096]{1,0:T(8,128)(2,1)S(1)}, bf16[32,4096]{1,0:T(8,128)(2,1)S(1)}, u32[]{:S(2)}, u32[]{:S(2)}) collective-permute-start(bf16[32,4096]{1,0:T(8,128)(2,1)S(1)} %get-tuple-element.161), channel_id=1, source_target_pairs={{0,2},{1,3},{4,0},{5,1},{8,4},{9,5},{12,8},{13,9},{14,12},{15,13},... | collective-permute-start | bytes 786440 | tf_op jit(solution)/shard_map/ppermute | solution.py:256
